TPU v7x, 256 devices: a whole 4x4x8 slice. The times are simulated.
256 devices in a mesh: dp: 8 (over y, core), label: 32 (over x, z).
Axes of the slice: x: 4, y: 4, z: 8, core: 2. Of those that a mesh axis runs over, the one named last changes fastest.
Arguments:
- encoded: bfloat16 [32768, 1024], P(('dp', 'label')), may hold values from -6 to 6
- positive_clusters: int32 [32768, 4], P(('dp', 'label')), may hold values from 0 to 16383
- cluster_weight: bfloat16 [16384, 1024], P('label'), may hold values from -0.1875 to 0.1875
- shortlist: int32 [32768, 4], P(('dp', 'label')), may hold values from 0 to 511, all different within a row; in each aligned block of 128 rows (0 to 127, 128 to 255, ...) at most 2 rows name the same one
- positive_offsets: int32 [32768, 4], P(('dp', 'label')), may hold values from 0 to 127
- block_weight: bfloat16 [512, 128, 1024], P('label'), may hold values from -0.1875 to 0.1875
Outputs:
- grad_hidden: bfloat16 [32768, 1024], P(('dp', 'label'))
- grad_cluster: float32 [16384, 1024], P('label', 'dp')
- grad_block: float32 [512, 128, 1024], P('label', None, 'dp')
Inputs may be any that keep to these rules, and one draw needn't show every extreme that they name: `shortlist`: each row names 4 different blocks. Among the rows of one device no block is named more than 2 times, and in every draw some block is named exactly 2 times by the rows of some device.
All inputs are finite; a program needn't handle non-finite values.
Results may differ from a plain program's by a relative error of at most 0.018.
Values may be sent and summed in bfloat16 or wider, within the bound.
A program may use at most 128 MiB of HBM per device.

v0:
```python
import math

import jax
import jax.numpy as jnp
from jax import lax
from jax.sharding import PartitionSpec as P


def per_device(
    encoded, positive_clusters, cluster_weight, shortlist, positive_offsets, block_weight
):
    doc_rows, width = encoded.shape
    label_count = lax.axis_size("label")
    label_index = lax.axis_index("label")
    clusters_dev = cluster_weight.shape[0]
    rows_all = doc_rows * label_count
    scale = 1.0 / math.sqrt(rows_all * lax.axis_size("dp"))
    cluster_ids = label_index * clusters_dev + jnp.arange(clusters_dev, dtype=jnp.int32)
    rows = lax.all_gather(encoded, "label", axis=0, tiled=True)
    positives = lax.all_gather(positive_clusters, "label", axis=0, tiled=True)
    scores = lax.dot_general(
        rows, cluster_weight, (((1,), (1,)), ((), ())), preferred_element_type=jnp.float32
    )
    hits = jnp.any(positives[:, :, None] == cluster_ids[None, None, :], axis=1)
    delta = (jax.nn.sigmoid(scores) - hits.astype(jnp.float32)).astype(jnp.bfloat16)
    grad_sum = lax.dot_general(
        delta, rows, (((0,), (0,)), ((), ())), preferred_element_type=jnp.float32
    )
    deltas = delta
    grad_cluster, deltas = (grad_sum, deltas)
    products = jnp.dot(deltas, cluster_weight, preferred_element_type=jnp.float32)
    hidden_one = lax.psum_scatter(
        products.astype(jnp.bfloat16), "label", scatter_dimension=0, tiled=True
    ).astype(jnp.float32)
    listed = shortlist.shape[1]
    pairs = doc_rows * listed
    blocks_dev, block_len, _ = block_weight.shape
    blocks_total = blocks_dev * label_count
    capacity = max(2, 2 * pairs // blocks_total)
    slots_total = blocks_total * capacity
    flat_block = shortlist.reshape(-1)
    onehot = (flat_block[:, None] == jnp.arange(blocks_total, dtype=jnp.int32)[None, :]).astype(
        jnp.bfloat16
    )
    lower = (jnp.arange(pairs)[:, None] > jnp.arange(pairs)[None, :]).astype(jnp.bfloat16)
    earlier = jnp.dot(lower, onehot, preferred_element_type=jnp.float32)
    rank = jnp.sum(earlier * onehot.astype(jnp.float32), axis=1).astype(jnp.int32)
    slot = flat_block * capacity + rank
    source = (
        jnp.full((slots_total,), -1, jnp.int32).at[slot].set(jnp.arange(pairs, dtype=jnp.int32))
    )
    filled = source >= 0
    picked = jnp.maximum(source, 0)
    send_rows = jnp.where(filled[:, None], encoded[picked // listed], jnp.zeros((), jnp.bfloat16))
    send_offsets = jnp.where(filled, positive_offsets.reshape(-1)[picked], -1)
    send_rows = send_rows.reshape(label_count, blocks_dev * capacity, width)
    send_offsets = send_offsets.reshape(label_count, blocks_dev * capacity)
    got_rows, got_offsets = (
        lax.all_to_all(send_rows, "label", split_axis=0, concat_axis=0, tiled=True),
        lax.all_to_all(send_offsets, "label", split_axis=0, concat_axis=0, tiled=True),
    )
    arrived = got_rows.reshape(label_count, blocks_dev, capacity, width)
    offsets = got_offsets.reshape(label_count, blocks_dev, capacity)
    scores = jnp.einsum("sbcd,bld->sbcl", arrived, block_weight, preferred_element_type=jnp.float32)
    target = (offsets[..., None] == jnp.arange(block_len, dtype=jnp.int32)).astype(jnp.float32)
    delta = jnp.where((offsets >= 0)[..., None], jax.nn.sigmoid(scores) - target, 0.0).astype(
        jnp.bfloat16
    )
    back = jnp.einsum(
        "sbcl,bld->sbcd", delta, block_weight, preferred_element_type=jnp.float32
    ).astype(jnp.bfloat16)
    grad_block = jnp.einsum("sbcl,sbcd->bld", delta, arrived, preferred_element_type=jnp.float32)
    returned = lax.all_to_all(
        back.reshape(label_count, blocks_dev * capacity, width),
        "label",
        split_axis=0,
        concat_axis=0,
        tiled=True,
    )
    per_pair = returned.reshape(slots_total, width)[slot].astype(jnp.float32)
    hidden_two = jnp.sum(per_pair.reshape(doc_rows, listed, width), axis=1)
    grad_hidden = (hidden_one + hidden_two).astype(jnp.bfloat16)
    cluster_share, block_share = (
        lax.psum_scatter(
            (grad_cluster * scale).astype(jnp.bfloat16), "dp", scatter_dimension=1, tiled=True
        ).astype(jnp.float32),
        lax.psum_scatter(
            (grad_block * scale).reshape(blocks_dev * block_len, width).astype(jnp.bfloat16),
            "dp",
            scatter_dimension=1,
            tiled=True,
        ).astype(jnp.float32),
    )
    return (grad_hidden, cluster_share, block_share.reshape(blocks_dev, block_len, -1))


def solution(mesh):
    placed = (
        P(("dp", "label"), None),
        P(("dp", "label"), None),
        P("label", None),
        P(("dp", "label"), None),
        P(("dp", "label"), None),
        P("label", None, None),
    )
    return jax.shard_map(
        per_device,
        mesh=mesh,
        in_specs=placed,
        out_specs=(P(("dp", "label"), None), P("label", "dp"), P("label", None, "dp")),
        check_vma=False,
    )
```

profile of v0, /device:TPU:2, one launch (start us, length us, event | category | flops | bytes accessed | tf_op | source)
XLA Modules:
  0.0 471.3 jit_solution(16597565565228183674)
XLA Ops:
  8.1 0.7 all-gather.2.cloned.1.call-update
  8.8 0.8 copy.38
  9.5 0.7 broadcast_multiply_fusion
  10.2 0.1 copy.37
  10.3 0.1 mul.37
  10.5 0.8 copy.39
  11.2 0.1 reshape.92
  11.4 0.1 eq.42
  11.5 0.5 fusion.8
  12.0 2.4 scatter_custom_fusion
  14.5 6.9 %gather_fusion = s32[1024]{0:T(1024)S(1)} fusion(s32[512]{0:T(512)S(1)} %reshape.92, s32[1024]{0:T(1024)S(1)} %maximum_clamp_fusion), kind=kCustom, calls=%fused_computation | custom fusion | bytes 12288 | tf_op jit(solution)/shard_map/gather | solution.py:55
  21.4 0.7 all_to_all.12
  22.1 11.6 %all-to-all-start = ((s32[32,1,32]{2,1,0:T(1,128)}), s32[32,1,32]{2,1,0:T(1,128)S(1)}, u32[]{:S(2)}, u32[]{:S(2)}) async-start(s32[32,1,32]{2,1,0:T(1,128)} %bitcast.2), calls=%async_computation.1 | async-start | bytes 32768 | tf_op jit(solution)/shard_map/all_to_all | solution.py:60
  33.7 0.1 broadcast_in_dim.50
  33.8 4.1 gather_fusion.1
  37.8 1.6 broadcast_select_fusion
  39.4 3.0 all-to-all-done
  42.4 6.8 %all-to-all-start.1 = ((bf16[32,32,1024]{2,1,0:T(8,128)(2,1)}), bf16[32,32,1024]{2,1,0:T(8,128)(2,1)S(1)}, u32[]{:S(2)}, u32[]{:S(2)}) async-start(bf16[32,32,1024]{2,1,0:T(8,128)(2,1)} %broadcast_select_fusion), calls=%async_computation.2 | async-start | bytes 4194304 | tf_op jit(solution)/shard_map/all_to_all | solution.py:59
  49.3 0.1 copy.41
  49.4 63.3 %all-to-all-done.1 = bf16[32,32,1024]{2,1,0:T(8,128)(2,1)S(1)} async-done(((bf16[32,32,1024]{2,1,0:T(8,128)(2,1)}), bf16[32,32,1024]{2,1,0:T(8,128)(2,1)S(1)}, u32[]{:S(2)}, u32[]{:S(2)}) %all-to-all-start.1) | async-done | bytes 2097184 | tf_op jit(solution)/shard_map/all_to_all | solution.py:59
  112.6 1.2 copy.42
  113.8 1.2 copy-done.2
  115.0 1.7 fusion.30
  116.7 3.2 fusion
  119.9 6.5 %copy.48 = bf16[2048,1024]{0,1:T(8,128)(2,1)} copy(bf16[2048,1024]{1,0:T(8,128)(2,1)} %bitcast.68) | data formatting | bytes 8388608
  126.5 0.0 reduce-scatter.10.cloned.1.call-start
  126.5 0.6 copy-done.3
  127.1 47.6 %all_gather.7 = s32[4096,4]{0,1:T(4,128)S(1)} all-gather(s32[128,4]{0,1:T(4,128)S(1)} %copy-done.3), channel_id=1, replica_groups=mesh['dp'=8,'label'=32] {'label'}, dimensions={0}, use_global_device_ids=true | all-gather | bytes 67584 | tf_op jit(solution)/shard_map/all_gather | solution.py:20
  174.8 5.1 %compare_reduce_fusion = pred[4096,512]{1,0:T(8,128)(4,1)S(1)} fusion(s32[512]{0:T(512)S(1)} %iota_add_fusion, s32[4096,4]{0,1:T(4,128)S(1)} %all_gather.7), kind=kLoop, calls=%fused_computation.4 | loop fusion | flops 14680064 | bytes 2164736 | tf_op jit(solution)/shard_map/reduce_or | solution.py:24
  180.0 9.2 %subtract_convert_fusion = bf16[4096,512]{1,0:T(8,128)(2,1)S(1)} fusion(pred[4096,512]{1,0:T(8,128)(4,1)S(1)} %compare_reduce_fusion, bf16[4096,1024]{1,0:T(8,128)(2,1)} %all-gather.2.cloned.1.call-done, bf16[512,1024]{1,0:T(8,128)(2,1)S(1)} %copy-done), kind=kOutput, calls=%fused_computation.7 | convolution fusion | flops 4307550208 | bytes 15728640 | tf_op jit(solution)/shard_map/dot_general | solution.py:21
  189.2 1.9 copy-done.5
  191.1 4.5 multiply_convert_fusion
  195.6 1.3 copy.46
  197.0 0.3 reduce-scatter.8.cloned.1.call-start
  197.2 9.0 %convolution_convert_fusion = bf16[4096,1024]{1,0:T(8,128)(2,1)} fusion(bf16[4096,512]{1,0:T(8,128)(2,1)} %copy-done.5, bf16[512,1024]{1,0:T(8,128)(2,1)S(1)} %copy-done), kind=kOutput, calls=%fused_computation.8 | convolution fusion | flops 4299161600 | bytes 13631488 | tf_op jit(solution)/shard_map/dot_general | solution.py:31
  206.3 2.9 fusion.5
  209.2 2.5 copy.43
  211.7 6.7 %all-to-all-start.2 = ((bf16[32,32,1024]{2,1,0:T(8,128)(2,1)}), bf16[32,32,1024]{2,1,0:T(8,128)(2,1)S(1)}, u32[]{:S(2)}, u32[]{:S(2)}) async-start(bf16[32,32,1024]{2,1,0:T(8,128)(2,1)} %copy.43), calls=%async_computation.3 | async-start | bytes 4194304 | tf_op jit(solution)/shard_map/all_to_all | solution.py:73
  218.4 41.4 %all-to-all-done.2 = bf16[32,32,1024]{2,1,0:T(8,128)(2,1)S(1)} async-done(((bf16[32,32,1024]{2,1,0:T(8,128)(2,1)}), bf16[32,32,1024]{2,1,0:T(8,128)(2,1)S(1)}, u32[]{:S(2)}, u32[]{:S(2)}) %all-to-all-start.2) | async-done | bytes 2097184 | tf_op jit(solution)/shard_map/all_to_all | solution.py:73
  259.8 2.8 gather_fusion.2
  262.6 1.7 reshape.99
  264.3 2.2 reduce_sum.19
  266.6 1.3 copy.49
  267.9 1.1 convert.2
  269.0 1.0 copy.47
  270.0 0.7 convert_element_type.83
  270.7 191.1 %reduce-scatter.8.cloned.1.call-done = bf16[128,1024]{1,0:T(8,128)(2,1)} async-done(((bf16[4096,1024]{1,0:T(8,128)(2,1)}), bf16[128,1024]{1,0:T(8,128)(2,1)}) %reduce-scatter.8.cloned.1.call-update) | async-done | bytes 262160 | tf_op jit(solution)/shard_map/reduce_scatter | solution.py:32
  461.9 1.9 add_convert_fusion
  (25 shorter events, 0.2 us)
Async XLA Ops:
  8.0 172.0 %copy-start = (bf16[512,1024]{1,0:T(8,128)(2,1)S(1)}, bf16[512,1024]{1,0:T(8,128)(2,1)}, u32[]{:S(2)}) copy-start(bf16[512,1024]{1,0:T(8,128)(2,1)} %param.8) | copy-start | bytes 3145732
  8.0 25.8 %copy-start.1 = (bf16[128,1024]{1,0:T(8,128)(2,1)S(1)}, bf16[128,1024]{1,0:T(8,128)(2,1)}, u32[]{:S(2)}) copy-start(bf16[128,1024]{1,0:T(8,128)(2,1)} %param.6) | copy-start | bytes 786436
  8.0 171.9 %all-gather.2.cloned.1.call-start = ((), (), s32[]{:S(2)}) async-start(), calls=%async_computation.6 | async-start | bytes 8650752 | tf_op jit(solution)/shard_map/all_gather | solution.py:19
  22.1 20.3 %all-to-all-start = ((s32[32,1,32]{2,1,0:T(1,128)}), s32[32,1,32]{2,1,0:T(1,128)S(1)}, u32[]{:S(2)}, u32[]{:S(2)}) async-start(s32[32,1,32]{2,1,0:T(1,128)} %bitcast.2), calls=%async_computation.1 | async-start | bytes 32768 | tf_op jit(solution)/shard_map/all_to_all | solution.py:60
  42.4 70.2 %all-to-all-start.1 = ((bf16[32,32,1024]{2,1,0:T(8,128)(2,1)}), bf16[32,32,1024]{2,1,0:T(8,128)(2,1)S(1)}, u32[]{:S(2)}, u32[]{:S(2)}) async-start(bf16[32,32,1024]{2,1,0:T(8,128)(2,1)} %broadcast_select_fusion), calls=%async_computation.2 | async-start | bytes 4194304 | tf_op jit(solution)/shard_map/all_to_all | solution.py:59
  49.2 217.3 %reduce-scatter.12.cloned.1.call-start = ((), (), s32[]{:S(2)}) async-start(), calls=%async_computation.9 | async-start | bytes 4718592
  112.6 2.3 copy-start.2
  126.4 0.7 copy-start.3
  126.5 142.5 %reduce-scatter.10.cloned.1.call-start = ((), (), s32[]{:S(2)}) async-start(), calls=%async_computation.8 | async-start | bytes 1179648
  180.0 11.1 %copy-start.4 = (bf16[4096,1024]{1,0:T(8,128)(2,1)S(1)}, bf16[4096,1024]{1,0:T(8,128)(2,1)}, u32[]{:S(2)}) copy-start(bf16[4096,1024]{1,0:T(8,128)(2,1)} %all-gather.2.cloned.1.call-done) | copy-start | bytes 25165828
  189.2 1.9 copy-start.5
  197.0 264.9 %reduce-scatter.8.cloned.1.call-start = ((), (), s32[]{:S(2)}) async-start(), calls=%async_computation.7 | async-start | bytes 8650752 | tf_op jit(solution)/shard_map/reduce_scatter | solution.py:32
  211.7 48.2 %all-to-all-start.2 = ((bf16[32,32,1024]{2,1,0:T(8,128)(2,1)}), bf16[32,32,1024]{2,1,0:T(8,128)(2,1)S(1)}, u32[]{:S(2)}, u32[]{:S(2)}) async-start(bf16[32,32,1024]{2,1,0:T(8,128)(2,1)} %copy.43), calls=%async_computation.3 | async-start | bytes 4194304 | tf_op jit(solution)/shard_map/all_to_all | solution.py:73
Sparse Core Ops, SparseCore 0:
  11.4 125.7 all-gather.1
Sparse Core Ops, SparseCore 1:
  126.6 38.5 reduce-scatter.11
  197.1 32.6 reduce-scatter.9
  233.6 228.2 reduce-scatter.7
where the time goes:
time: 473 us; the launch traced here: 471 us
  waiting for transfers between devices  300 us (63%)
  blocking collectives  47.6 us (10%)
  local copies, waits for them, and re-layouts  38.2 us (8%)
  matrix products  31.1 us (7%)
  starting transfers between devices  25.6 us (5%)
  between operations  15.9 us (3%)
  other arithmetic  13.4 us (3%)
    reduce_scatter x1, waiting for transfers between devices, per_device(): lax.psum_scatter(products.astype(jnp.bfloat16), 'label', scatter_dimensio...  191 us
    all_to_all x1, waiting for transfers between devices, per_device(): lax.all_to_all(send_rows, 'label', split_axis=0, concat_axis=0, tiled=True)  63.3 us
    all_gather x1, blocking collectives, per_device(): positives = lax.all_gather(positive_clusters, 'label', axis=0, tiled=True)  47.6 us
    all_to_all x1, waiting for transfers between devices, per_device(): lax.all_to_all(back.reshape(label_count, blocks_dev * capacity, width), '...  41.4 us
    unnamed x18, local copies, waits for them, and re-layouts  15.5 us
    all_to_all x1, starting transfers between devices, per_device(): lax.all_to_all(send_offsets, 'label', split_axis=0, concat_axis=0, tiled=...  11.6 us
  transfers between devices with their start and end apart: 7, of which 4 were waited for; matrix products, arithmetic and copies ran while one was open for 16% of the time, Pallas kernels for 0%

commit v1 on v0

v1 whole, which is shorter than its diff:
```python
import math

import jax
import jax.numpy as jnp
from jax import lax
from jax.experimental import pallas as pl
from jax.experimental.pallas import tpu as pltpu
from jax.sharding import PartitionSpec as P

MESH = pl.DeviceIdType.MESH
F32, BF16 = jnp.float32, jnp.bfloat16
NY, NC, NX, NZ = 4, 2, 4, 8
DOC, D, CL, LBL = 128, 1024, 512, 128
VMEM_LIMIT = 60 * 1024 * 1024


class Spot:
    def __init__(self):
        dp, label = lax.axis_index("dp"), lax.axis_index("label")
        self.y, self.c = dp // NC, dp % NC
        self.x, self.z = label // NZ, label % NZ

    def at(self, dx=0, dy=0, dz=0, dc=0):
        y, x, z = (self.y + dy) % NY, (self.x + dx) % NX, (self.z + dz) % NZ
        return (y * NC + (self.c + dc) % NC, x * NZ + z)


def greet(others):
    barrier = pltpu.get_barrier_semaphore()
    for other in others:
        pl.semaphore_signal(barrier, inc=1, device_id=other, device_id_type=MESH)
    pl.semaphore_wait(barrier, len(others))


class Copies:
    def __init__(self, send, recv):
        self.send, self.recv, self.used, self.sent = send, recv, 0, []

    def start(self, src, dst, device):
        i = self.used
        self.used += 1
        copy = pltpu.make_async_remote_copy(
            src_ref=src, dst_ref=dst, send_sem=self.send.at[i], recv_sem=self.recv.at[i],
            device_id=device, device_id_type=MESH,
        )
        copy.start()
        self.sent.append(copy)
        return copy

    def finish(self):
        for copy in self.sent:
            copy.wait_send()


def dot(a, b, dims):
    return lax.dot_general(a, b, (dims, ((), ())), preferred_element_type=F32)


def gather_kernel(enc, w, meta, docs, wrel, metas, arr, tgt, place, disp, send, recv, local):
    me = Spot()
    x, y, z, c = me.x, me.y, me.z, me.c
    greet(
        [me.at(dz=i) for i in range(1, NZ)] + [me.at(dx=i) for i in range(1, NX)]
        + [me.at(dy=1), me.at(dy=-1), me.at(dc=1)]
    )
    cp = Copies(send, recv)
    half = DOC // 2
    right = cp.start(enc, docs.at[z], me.at(dz=1))
    left = cp.start(enc, docs.at[z], me.at(dz=-1))
    got_meta = [None] + [cp.start(meta, metas.at[z], me.at(dz=i)) for i in range(1, NZ)]
    w_right = cp.start(w.at[y, c], wrel.at[3, y, c], me.at(dx=1))
    w_left = cp.start(w.at[y, c], wrel.at[1, y, c], me.at(dx=-1))
    own = [
        pltpu.make_async_copy(w, wrel.at[0], local.at[0]),
        pltpu.make_async_copy(enc, docs.at[z], local.at[1]),
        pltpu.make_async_copy(meta, metas.at[z], local.at[2]),
    ]
    for copy in own:
        copy.start()

    slot = lax.broadcasted_iota(jnp.int32, (128, 128), 0)
    block = (((x + (slot >> 5)) & 3) * NZ + z) * 16 + (slot & 15)
    turn = ((slot >> 4) & 1).astype(F32)
    lane = lax.broadcasted_iota(jnp.int32, (128, 128), 1)
    upper = jnp.where(slot < lane, 1.0, 0.0).astype(BF16)
    row8 = lax.broadcasted_iota(jnp.int32, (8, 128), 0)
    tgt[0] = jnp.zeros((8, 128), F32)
    arrivals = []

    def dispatch(zs):
        info = metas[zs]
        named = jnp.zeros((128, 128), F32)
        offset = jnp.zeros((128, 128), F32)
        for k in range(4):
            hit = info[4 + k:5 + k, :] == block
            named = jnp.where(hit, 1.0, named)
            offset = jnp.where(hit, (info[8 + k:9 + k, :] + 1).astype(F32), offset)
        rank = dot(named.astype(BF16), upper, ((1,), (0,)))
        chosen = jnp.where(rank == turn, named, 0.0)
        place[zs] = chosen.astype(BF16)
        disp[zs] = dot(chosen.astype(BF16), docs[zs], ((1,), (0,))).astype(BF16)
        pick = jnp.where(row8 == zs, 1.0, 0.0).astype(BF16)
        tgt[0] += dot(pick, (chosen * offset).astype(BF16), ((1,), (1,)))
        for d in range(1, NX):
            arrivals.append(
                cp.start(disp.at[zs, pl.ds(d * 32, 32)], arr.at[NX - d, zs], me.at(dx=d))
            )
        arr[0, zs] = disp[zs, 0:32]

    own[1].wait()
    own[2].wait()
    dispatch(z)
    groups = pl.ds(1, 3)
    for h in range(1, NZ // 2):
        from_left, from_right = (z - h) % NZ, (z + h) % NZ
        right.wait_recv()
        left.wait_recv()
        if h + 1 < NZ // 2:
            right = cp.start(docs.at[from_left], docs.at[from_left], me.at(dz=1))
            left = cp.start(docs.at[from_right], docs.at[from_right], me.at(dz=-1))
        else:
            right = cp.start(
                docs.at[from_left, pl.ds(0, half)], docs.at[from_left, pl.ds(0, half)], me.at(dz=1)
            )
            left = cp.start(
                docs.at[from_right, pl.ds(half, half)], docs.at[from_right, pl.ds(half, half)], me.at(dz=-1)
            )
        if h == 1:
            w_right.wait_recv()
            w_left.wait_recv()
            w_right = cp.start(w_part(wrel, 3, y, c, 0), w_part(wrel, 2, y, c, 0), me.at(dx=1))
            w_left = cp.start(w_part(wrel, 1, y, c, 1), w_part(wrel, 2, y, c, 1), me.at(dx=-1))
        if h == 2:
            w_right.wait_recv()
            w_left.wait_recv()
            y_right = cp.start(wrel.at[groups, y, c], wrel.at[groups, y, c], me.at(dy=1))
            y_left = cp.start(wrel.at[groups, y, c], wrel.at[groups, y, c], me.at(dy=-1))
            sib = [cp.start(wrel.at[groups, y, c], wrel.at[groups, y, c], me.at(dc=1))]
        if h == 3:
            y_right.wait_recv()
            y_left.wait_recv()
            yl, yr = (y - 1) % NY, (y + 1) % NY
            sib.append(cp.start(wrel.at[groups, yl, c], wrel.at[groups, yl, c], me.at(dc=1)))
            sib.append(cp.start(wrel.at[groups, yr, c], wrel.at[groups, yr, c], me.at(dc=1)))
            a, b = pl.ds(0, 32), pl.ds(32, 32)
            y_right = cp.start(wrel.at[groups, yl, c, a], wrel.at[groups, yl, c, a], me.at(dy=1))
            y_left = cp.start(wrel.at[groups, yr, c, b], wrel.at[groups, yr, c, b], me.at(dy=-1))
        got_meta[h].wait_recv()
        dispatch(from_left)
        got_meta[NZ - h].wait_recv()
        dispatch(from_right)
    y_right.wait_recv()
    y_left.wait_recv()
    far = (y + 2) % NY
    sib.append(cp.start(wrel.at[groups, far, c], wrel.at[groups, far, c], me.at(dc=1)))
    right.wait_recv()
    left.wait_recv()
    got_meta[NZ // 2].wait_recv()
    dispatch((z + NZ // 2) % NZ)
    for d in range(1, NX):
        arrivals.append(cp.start(tgt.at[0], tgt.at[NX - d], me.at(dx=d)))
    for copy in arrivals + sib:
        copy.wait_recv()
    own[0].wait()
    cp.finish()


def w_part(wrel, group, y, c, part):
    return wrel.at[group, y, c, pl.ds(part * 32, 32)]


def gather(enc, w, meta):
    vmem = pl.BlockSpec(memory_space=pltpu.VMEM)
    copies = 64
    return pl.pallas_call(
        gather_kernel,
        out_shape=(
            jax.ShapeDtypeStruct((NZ, DOC, D), BF16),
            jax.ShapeDtypeStruct((NX, NY, NC, 64, D), BF16),
            jax.ShapeDtypeStruct((NZ, 16, 128), jnp.int32),
            jax.ShapeDtypeStruct((NX, NZ, 32, D), BF16),
            jax.ShapeDtypeStruct((NX, NZ, 128), F32),
            jax.ShapeDtypeStruct((NZ, 128, 128), BF16),
        ),
        in_specs=[vmem] * 3,
        out_specs=(vmem,) * 6,
        scratch_shapes=[
            pltpu.VMEM((NZ, 128, D), BF16),
            pltpu.SemaphoreType.DMA((copies,)),
            pltpu.SemaphoreType.DMA((copies,)),
            pltpu.SemaphoreType.DMA((3,)),
        ],
        compiler_params=pltpu.CompilerParams(
            collective_id=0, has_side_effects=True, vmem_limit_bytes=VMEM_LIMIT
        ),
    )(enc, w.reshape(NY, NC, 64, D), meta)


def reduce_kernel(
    back, place, hidden, gc, gb, out_h, out_c, out_b,
    ret, hid, zs_r, zs_l, zr_r, zr_l,
    c_in, c_sum, x_r2, x_l2, x_s, x_r, x_y, cy_2, cy_s, cy_r,
    b_in, b_sum, by_2, by_s, by_r, send, recv,
):
    me = Spot()
    x, y, z, c = me.x, me.y, me.z, me.c
    greet(
        [me.at(dx=i) for i in range(1, NX)]
        + [me.at(dz=1), me.at(dz=-1), me.at(dy=1), me.at(dy=-1), me.at(dc=1)]
    )
    cp = Copies(send, recv)
    returns = [
        cp.start(back.at[e], ret.at[pl.ds(0, NZ), pl.ds((NX - e) * 32, 32)], me.at(dx=e)) for e in range(1, NX)
    ]
    b_core = cp.start(gb.at[pl.ds(0, NY), 1 - c], b_in, me.at(dc=1))
    c_core = cp.start(gc.at[pl.ds(0, NY), 1 - c], c_in, me.at(dc=1))
    for i in range(NZ):
        ret[i, 0:32] = back[0, i]

    b_core.wait_recv()

    def add_block(i, carry):
        rows = pl.ds(pl.multiple_of((i % 4) * 512, 512), 512)
        b_sum[i // 4, rows] = (gb[i // 4, c, rows].astype(F32) + b_in[i // 4, rows].astype(F32)).astype(BF16)
        return carry

    lax.fori_loop(0, 16, add_block, 0)
    top, low = pl.ds(0, 1024), pl.ds(1024, 1024)
    far = (y + 2) % NY
    b_right = cp.start(b_sum.at[far, top], by_2.at[top], me.at(dy=1))
    b_left = cp.start(b_sum.at[far, low], by_2.at[low], me.at(dy=-1))

    c_core.wait_recv()

    def add_cluster(i, carry):
        g, t = i // 4, i % 4
        c_sum[g, t] = (gc[t, c, g].astype(F32) + c_in[t, g].astype(F32)).astype(BF16)
        return carry

    lax.fori_loop(0, 16, add_cluster, 0)
    x_right = cp.start(c_sum.at[2, pl.ds(0, 2)], x_r2, me.at(dx=1))
    x_left = cp.start(c_sum.at[2, pl.ds(2, 2)], x_l2, me.at(dx=-1))

    for copy in returns:
        copy.wait_recv()

    def combine(t):
        hid[t] = hidden[t] + dot(place[t], ret[t], ((0,), (0,)))

    half = DOC // 2
    t = (z + 4) % NZ
    combine(t)
    zs_r[3, 0:half] = hid[t, 0:half].astype(BF16)
    zs_l[3, half:DOC] = hid[t, half:DOC].astype(BF16)
    a, b = pl.ds(0, half), pl.ds(half, half)
    z_right = cp.start(zs_r.at[3, a], zr_r.at[3, a], me.at(dz=1))
    z_left = cp.start(zs_l.at[3, b], zr_l.at[3, b], me.at(dz=-1))

    def z_step(h):
        right, left = (z + h) % NZ, (z - h) % NZ
        combine(right)
        combine(left)
        z_right.wait_recv()
        z_left.wait_recv()
        if h == 3:
            zs_r[2, 0:half] = (hid[right, 0:half] + zr_r[3, 0:half].astype(F32)).astype(BF16)
            zs_r[2, half:DOC] = hid[right, half:DOC].astype(BF16)
            zs_l[2, half:DOC] = (hid[left, half:DOC] + zr_l[3, half:DOC].astype(F32)).astype(BF16)
            zs_l[2, 0:half] = hid[left, 0:half].astype(BF16)
        else:
            zs_r[h - 1] = (hid[right] + zr_r[h].astype(F32)).astype(BF16)
            zs_l[h - 1] = (hid[left] + zr_l[h].astype(F32)).astype(BF16)
        return (
            cp.start(zs_r.at[h - 1], zr_r.at[h - 1], me.at(dz=1)),
            cp.start(zs_l.at[h - 1], zr_l.at[h - 1], me.at(dz=-1)),
        )

    z_right, z_left = z_step(3)

    x_right.wait_recv()
    x_left.wait_recv()

    def add_x(i, carry):
        x_s[0, i] = (c_sum[1, i].astype(F32) + x_r2[i].astype(F32)).astype(BF16)
        x_s[0, i + 2] = c_sum[1, i + 2]
        x_s[1, i + 2] = (c_sum[3, i + 2].astype(F32) + x_l2[i].astype(F32)).astype(BF16)
        x_s[1, i] = c_sum[3, i]
        return carry

    lax.fori_loop(0, 2, add_x, 0)
    x_right = cp.start(x_s.at[0], x_r.at[0], me.at(dx=1))
    x_left = cp.start(x_s.at[1], x_r.at[1], me.at(dx=-1))

    b_right.wait_recv()
    b_left.wait_recv()
    up, down = (y + 1) % NY, (y - 1) % NY

    def add_b(i, carry):
        rows = pl.ds(pl.multiple_of(i * 512, 512), 512)
        other = pl.ds(pl.multiple_of(i * 512 + 1024, 512), 512)
        by_s[0, rows] = (b_sum[up, rows].astype(F32) + by_2[rows].astype(F32)).astype(BF16)
        by_s[0, other] = b_sum[up, other]
        by_s[1, other] = (b_sum[down, other].astype(F32) + by_2[other].astype(F32)).astype(BF16)
        by_s[1, rows] = b_sum[down, rows]
        return carry

    lax.fori_loop(0, 2, add_b, 0)
    b_right = cp.start(by_s.at[0], by_r.at[0], me.at(dy=1))
    b_left = cp.start(by_s.at[1], by_r.at[1], me.at(dy=-1))

    z_right, z_left = z_step(2)

    x_right.wait_recv()
    x_left.wait_recv()

    def add_x2(i, carry):
        x_y[i] = (c_sum[0, i].astype(F32) + x_r[0, i].astype(F32) + x_r[1, i].astype(F32)).astype(BF16)
        return carry

    lax.fori_loop(0, NY, add_x2, 0)
    ct, cl = pl.ds(0, 256), pl.ds(256, 256)
    c_right = cp.start(x_y.at[far, ct], cy_2.at[ct], me.at(dy=1))
    c_left = cp.start(x_y.at[far, cl], cy_2.at[cl], me.at(dy=-1))

    z_right, z_left = z_step(1)

    c_right.wait_recv()
    c_left.wait_recv()
    cy_s[0, ct] = (x_y[up, ct].astype(F32) + cy_2[ct].astype(F32)).astype(BF16)
    cy_s[0, cl] = x_y[up, cl]
    cy_s[1, cl] = (x_y[down, cl].astype(F32) + cy_2[cl].astype(F32)).astype(BF16)
    cy_s[1, ct] = x_y[down, ct]
    c_right = cp.start(cy_s.at[0], cy_r.at[0], me.at(dy=1))
    c_left = cp.start(cy_s.at[1], cy_r.at[1], me.at(dy=-1))

    combine(z)
    b_right.wait_recv()
    b_left.wait_recv()

    def add_b2(i, carry):
        rows = pl.ds(pl.multiple_of(i * 512, 512), 512)
        out_b[rows] = b_sum[y, rows].astype(F32) + by_r[0, rows].astype(F32) + by_r[1, rows].astype(F32)
        return carry

    lax.fori_loop(0, 4, add_b2, 0)
    z_right.wait_recv()
    z_left.wait_recv()
    out_h[...] = (hid[z] + zr_r[0].astype(F32) + zr_l[0].astype(F32)).astype(BF16)
    c_right.wait_recv()
    c_left.wait_recv()
    out_c[...] = x_y[y].astype(F32) + cy_r[0].astype(F32) + cy_r[1].astype(F32)
    cp.finish()


def reduce(back, place, hidden, gc, gb):
    vmem = pl.BlockSpec(memory_space=pltpu.VMEM)
    copies = 32
    bf = lambda *shape: pltpu.VMEM(shape, BF16)
    return pl.pallas_call(
        reduce_kernel,
        out_shape=(
            jax.ShapeDtypeStruct((DOC, D), BF16),
            jax.ShapeDtypeStruct((CL, 128), F32),
            jax.ShapeDtypeStruct((2048, 128), F32),
        ),
        in_specs=[vmem] * 5,
        out_specs=(vmem,) * 3,
        scratch_shapes=[
            bf(NZ, 128, D), pltpu.VMEM((NZ, DOC, D), F32),
            bf(4, DOC, D), bf(4, DOC, D), bf(4, DOC, D), bf(4, DOC, D),
            bf(NY, NX, CL, 128), bf(NX, NY, CL, 128), bf(2, CL, 128), bf(2, CL, 128),
            bf(2, NY, CL, 128), bf(2, NY, CL, 128), bf(NY, CL, 128), bf(CL, 128), bf(2, CL, 128), bf(2, CL, 128),
            bf(NY, 2048, 128), bf(NY, 2048, 128), bf(2048, 128), bf(2, 2048, 128), bf(2, 2048, 128),
            pltpu.SemaphoreType.DMA((copies,)),
            pltpu.SemaphoreType.DMA((copies,)),
        ],
        compiler_params=pltpu.CompilerParams(
            collective_id=1, has_side_effects=True, vmem_limit_bytes=VMEM_LIMIT
        ),
    )(back, place, hidden, gc, gb)


def per_device(encoded, positive_clusters, cluster_weight, shortlist, positive_offsets, block_weight):
    scale = 1.0 / math.sqrt(DOC * NY * NC * NX * NZ)
    label = lax.axis_index("label")
    x, z = label // NZ, label % NZ
    meta = jnp.concatenate(
        [positive_clusters.T, shortlist.T, positive_offsets.T, jnp.zeros((4, DOC), jnp.int32)], axis=0
    )
    docs, wrel, metas, arr, tgt, place = gather(encoded, cluster_weight, meta)
    rows = docs.reshape(NZ * DOC, D)
    weight = wrel.reshape(NX * CL, D)
    scores = dot(rows, weight, ((1,), (1,)))
    group = (x + jnp.arange(NX, dtype=jnp.int32)) % NX * NZ + z
    ids = (group[:, None] * CL + jnp.arange(CL, dtype=jnp.int32)[None, :]).reshape(-1)
    positives = metas[:, 0:4, :].transpose(0, 2, 1).reshape(NZ * DOC, 4)
    hits = jnp.any(positives[:, :, None] == ids[None, None, :], axis=1)
    delta = (jax.nn.sigmoid(scores) - hits.astype(F32)).astype(BF16)
    grad_c = (dot(delta, rows, ((0,), (0,))) * scale).astype(BF16)
    hidden = dot(delta, weight, ((1,), (0,))).reshape(NZ, DOC, D)

    own = jnp.stack([tgt[e][:, ((NX - e) % NX) * 32:((NX - e) % NX) * 32 + 32] for e in range(NX)])
    own = own.reshape(NX, NZ, 2, 16).transpose(3, 0, 1, 2).reshape(16, 64).astype(jnp.int32)
    arrived = arr.reshape(NX, NZ, 2, 16, D).transpose(3, 0, 1, 2, 4).reshape(16, 64, D)
    scores = jnp.einsum("bsd,bld->bsl", arrived, block_weight, preferred_element_type=F32)
    target = (own[..., None] - 1 == jnp.arange(LBL, dtype=jnp.int32)).astype(F32)
    delta = jnp.where((own > 0)[..., None], jax.nn.sigmoid(scores) - target, 0.0).astype(BF16)
    back = jnp.einsum("bsl,bld->bsd", delta, block_weight, preferred_element_type=F32).astype(BF16)
    grad_b = jnp.einsum("bsl,bsd->bld", delta, arrived, preferred_element_type=F32)
    back = back.reshape(16, NX, NZ, 2, D).transpose(1, 2, 3, 0, 4).reshape(NX, NZ, 32, D)
    grad_b = (grad_b * scale).astype(BF16).reshape(2048, NY, NC, 128).transpose(1, 2, 0, 3)
    grad_c = grad_c.reshape(NX, CL, NY, NC, 128).transpose(2, 3, 0, 1, 4)
    out_h, out_c, out_b = reduce(back, place, hidden, grad_c, grad_b)
    return out_h, out_c, out_b.reshape(16, LBL, 128)


def solution(mesh):
    placed = (
        P(("dp", "label"), None),
        P(("dp", "label"), None),
        P("label", None),
        P(("dp", "label"), None),
        P(("dp", "label"), None),
        P("label", None, None),
    )
    return jax.shard_map(
        per_device,
        mesh=mesh,
        in_specs=placed,
        out_specs=(P(("dp", "label"), None), P("label", "dp"), P("label", None, "dp")),
        check_vma=False,
    )
```

time: 473 us -> 190 us (0.40)
  the two profiles are of different devices: /device:TPU:2 before, /device:TPU:8 now
where the time goes in v1:
time: 190 us
  Pallas kernels  112 us (59%)
  local copies, waits for them, and re-layouts  35.9 us (19%)
  matrix products  31.4 us (17%)
  other arithmetic  9.65 us (5%)
    pallas_call x1, Pallas kernels, reduce(): pl.pallas_call(reduce_kernel, out_shape=(jax.ShapeDtypeStruct((DOC, D), B...  62.8 us
    pallas_call x1, Pallas kernels, gather(): pl.pallas_call(gather_kernel, out_shape=(jax.ShapeDtypeStruct((NZ, DOC, D...  49.2 us
    dot_general x3, matrix products, dot(): return lax.dot_general(a, b, (dims, ((), ())), preferred_element_type=F32)  20.7 us
    reshape x2, local copies, waits for them, and re-layouts, per_device(): grad_c = grad_c.reshape(NX, CL, NY, NC, 128).transpose(2, 3, 0, 1, 4)  13 us
    reshape x2, local copies, waits for them, and re-layouts, per_device(): (grad_b * scale).astype(BF16).reshape(2048, NY, NC, 128)  12.6 us
    reduce_or x1, other arithmetic, per_device(): hits = jnp.any(positives[:, :, None] == ids[None, None, :], axis=1)  8.11 us
    unnamed x12, local copies, waits for them, and re-layouts  5.65 us
    dot_general x1, matrix products, per_device(): jnp.einsum('bsl,bsd->bld', delta, arrived, preferred_element_type=F32)  5.37 us

profile of v1, /device:TPU:8, one launch (start us, length us, event | category | flops | bytes accessed | tf_op | source)
XLA Modules:
  0.0 189.7 jit_solution(7038594957070026172)
XLA Ops:
  0.7 0.1 pad.7.clone
  0.8 1.4 add_add_fusion.meta
  2.1 0.1 add_bitcast_fusion
  2.2 49.2 %shard_map.85 = (bf16[8,128,1024]{2,1,0:T(8,128)(2,1)}, bf16[4,4,2,64,1024]{4,3,2,1,0:T(8,128)(2,1)}, s32[8,16,128]{2,1,0:T(8,128)}, bf16[4,8,32,1024]{3,2,1,0:T...) custom-call(bf16[128,1024]{1,0:T(8,128)(2,1)} %enc.1, bf16[4,2,64,1024]{3,2,1,0:T(8,128)(2,1)} %bitcast.64, ...), custom_call_target="tpu_custom_call" | custom-call | tf_op jit(solution)/shard_map/pallas_call | solution.py:175
  51.4 0.7 slice_bitcast_fusion.4
  52.1 0.1 stack.15
  52.2 0.1 slice.34
  52.2 0.1 stack.18
  52.3 0.1 slice.32
  52.4 0.1 stack.17
  52.5 0.1 slice.30
  52.5 0.1 stack.16
  52.7 0.1 copy.21
  52.8 0.1 copy.23
  52.9 0.8 slice_bitcast_fusion
  53.6 4.7 %fusion.21 = bf16[16,64,128]{2,1,0:T(8,128)(2,1)S(1)} fusion(bf16[16,128,1024]{2,1,0:T(8,128)(2,1)} %param.11, bf16[16,64,1024]{2,0,1:T(8,128)(2,1)} %bitcast.62, s32[16,64]{1,0:T(8,128)S(1)} %copy.23, pred[16,64]{1,0:T(8,128)(4,1)S(1)} %copy.21), kind=kOutput, calls=%fused_computation.16 | convolution fusion | flops 269484032 | bytes 6558720 | tf_op jit(solution)/shard_map/bsd,bld->bsl/dot_general | solution.py:405
  58.3 8.1 %compare_reduce_fusion = pred[1024,2048]{1,0:T(8,128)(4,1)S(1)} fusion(s32[2048]{0:T(1024)S(1)} %bitcast.67, s32[1024,4]{0,1:T(4,128)S(1)} %slice_bitcast_fusion), kind=kLoop, calls=%fused_computation | loop fusion | flops 14680064 | bytes 2121728 | tf_op jit(solution)/shard_map/reduce_or | solution.py:397
  66.5 0.0 copy-start.2
  66.5 8.4 %subtract_convert_fusion = bf16[1024,2048]{1,0:T(8,128)(2,1)S(1)} fusion(pred[1024,2048]{1,0:T(8,128)(4,1)S(1)} %compare_reduce_fusion, bf16[1024,1024]{1,0:T(8,128)(2,1)} %bitcast.74, bf16[2048,1024]{1,0:T(8,128)(2,1)} %bitcast.72), kind=kOutput, calls=%fused_computation.3 | convolution fusion | flops 4307550208 | bytes 12582912 | tf_op jit(solution)/shard_map/dot_general | solution.py:56
  74.9 0.0 copy-done.2
  74.9 0.0 copy-start.3
  74.9 6.0 %fusion.28.hidden = f32[8,128,1024]{2,1,0:T(8,128)} fusion(bf16[8,128,2048]{2,1,0:T(8,128)(2,1)S(1)} %bitcast.76, bf16[2048,1024,1]{1,0,2:T(8,128)(2,1)S(1)} %bitcast.73), kind=kOutput, calls=%fused_computation.35 | convolution fusion | flops 4294967296 | bytes 12582912 | tf_op jit(solution)/shard_map/dot_general | solution.py:56
  80.9 0.0 copy-done.3
  80.9 6.2 %multiply_convert_fusion.1 = bf16[2048,1024]{1,0:T(8,128)(2,1)} fusion(bf16[1024,2048]{1,0:T(8,128)(2,1)S(1)} %subtract_convert_fusion, bf16[1024,1024]{1,0:T(8,128)(2,1)S(1)} %bitcast.75), kind=kOutput, calls=%fused_computation.2 | convolution fusion | flops 4299161600 | bytes 10485760 | tf_op jit(solution)/shard_map/dot_general | solution.py:56
  87.2 7.8 %reshape.105 = bf16[4,512,4,2,128]{4,3,2,1,0:T(2,128)(2,1)} reshape(bf16[2048,1024]{1,0:T(8,128)(2,1)} %multiply_convert_fusion.1) | data formatting | bytes 8388608 | tf_op jit(solution)/shard_map/reshape | solution.py:412
  94.9 0.0 copy-start.1
  94.9 5.2 %copy.54 = bf16[4,512,4,2,128]{4,1,0,3,2:T(8,128)(2,1)} copy(bf16[4,512,4,2,128]{4,3,2,1,0:T(2,128)(2,1)} %reshape.105) | data formatting | bytes 8388608 | tf_op jit(solution)/shard_map/reshape | solution.py:412
  100.1 0.0 copy-done.1
  100.2 5.4 %multiply_convert_fusion = bf16[16,128,1024]{2,1,0:T(8,128)(2,1)} fusion(bf16[16,64,128]{2,1,0:T(8,128)(2,1)S(1)} %fusion.21, bf16[16,64,1024]{2,0,1:T(8,128)(2,1)S(1)} %bitcast.63), kind=kOutput, calls=%fused_computation.1 | convolution fusion | flops 272629760 | bytes 6553600 | tf_op jit(solution)/shard_map/bsl,bsd->bld/dot_general | solution.py:409
  105.5 7.7 %reshape.109 = bf16[2048,4,2,128]{3,2,1,0:T(2,128)(2,1)} reshape(bf16[16,128,1024]{2,1,0:T(8,128)(2,1)} %multiply_convert_fusion) | data formatting | bytes 8388608 | tf_op jit(solution)/shard_map/reshape | solution.py:411
  113.3 0.0 copy-start
  113.3 4.8 %copy.53 = bf16[2048,4,2,128]{3,0,2,1:T(8,128)(2,1)} copy(bf16[2048,4,2,128]{3,2,1,0:T(2,128)(2,1)} %reshape.109) | data formatting | bytes 8388608 | tf_op jit(solution)/shard_map/reshape | solution.py:411
  118.1 0.0 copy-done
  118.1 0.7 convolution_convert_fusion
  118.8 2.5 %copy.29 = bf16[16,64,1024]{2,0,1:T(8,128)(2,1)} copy(bf16[16,64,1024]{2,1,0:T(8,128)(2,1)S(1)} %convolution_convert_fusion) | data formatting | bytes 4194304 | tf_op jit(solution)/shard_map/reshape | solution.py:410
  121.3 62.8 %shard_map.86 = (bf16[128,1024]{1,0:T(8,128)(2,1)}, f32[512,128]{1,0:T(8,128)}, f32[2048,128]{1,0:T(8,128)}) custom-call(bf16[4,8,32,1024]{3,2,1,0:T(8,128)(2,1)} %bitcast.61, bf16[8,128,128]{2,1,0:T(8,128)(2,1)} %get-tuple-element.14.place, f32[8,128,1024]{2,1,0:T(8,128)} %fusion.28.hidden, bf16[4,2,4,512,128]{4,3,2,1,0:T(8,128)(2,1)} %bitcast.59, ...), custom_call_target="tpu_custom_call" | custom-call | tf_op jit(solution)/shard_map/pallas_call | solution.py:359
  184.1 1.7 copy.58
  185.8 1.7 copy.59
  187.4 2.3 %copy.60 = f32[16,128,128]{2,1,0:T(8,128)} copy(f32[16,128,128]{2,1,0:T(8,128)} %bitcast.65) | data formatting | bytes 2097152
  (6 shorter events, 0.1 us)
Async XLA Ops:
  66.5 8.4 %copy-start.2 = (bf16[4,4,2,64,1024]{4,3,2,1,0:T(8,128)(2,1)S(1)}, bf16[4,4,2,64,1024]{4,3,2,1,0:T(8,128)(2,1)}, u32[]{:S(2)}) copy-start(bf16[4,4,2,64,1024]{4,3,2,1,0:T(8,128)(2,1)} %get-tuple-element.16) | copy-start | bytes 12582916
  74.9 6.0 %copy-start.3 = (bf16[8,128,1024]{2,1,0:T(8,128)(2,1)S(1)}, bf16[8,128,1024]{2,1,0:T(8,128)(2,1)}, u32[]{:S(2)}) copy-start(bf16[8,128,1024]{2,1,0:T(8,128)(2,1)} %get-tuple-element.15) | copy-start | bytes 6291460
  94.9 5.2 %copy-start.1 = (bf16[4,8,32,1024]{3,2,1,0:T(8,128)(2,1)S(1)}, bf16[4,8,32,1024]{3,2,1,0:T(8,128)(2,1)}, u32[]{:S(2)}) copy-start(bf16[4,8,32,1024]{3,2,1,0:T(8,128)(2,1)} %get-tuple-element.13) | copy-start | bytes 6291460
  113.3 4.8 %copy-start = (bf16[16,128,1024]{2,1,0:T(8,128)(2,1)S(1)}, bf16[16,128,1024]{2,1,0:T(8,128)(2,1)}, u32[]{:S(2)}) copy-start(bf16[16,128,1024]{2,1,0:T(8,128)(2,1)} %param.11) | copy-start | bytes 12582916

commit v2 on v1

v2 whole, which is shorter than its diff:
```python
import math

import jax
import jax.numpy as jnp
from jax import lax
from jax.experimental import pallas as pl
from jax.experimental.pallas import tpu as pltpu
from jax.sharding import PartitionSpec as P

MESH = pl.DeviceIdType.MESH
F32, BF16 = jnp.float32, jnp.bfloat16
NY, NC, NX, NZ = 4, 2, 4, 8
DOC, D, CL, LBL = 128, 1024, 512, 128
VMEM_LIMIT = 60 * 1024 * 1024


class Spot:
    def __init__(self):
        dp, label = lax.axis_index("dp"), lax.axis_index("label")
        self.y, self.c = dp // NC, dp % NC
        self.x, self.z = label // NZ, label % NZ

    def at(self, dx=0, dy=0, dz=0, dc=0):
        y, x, z = (self.y + dy) % NY, (self.x + dx) % NX, (self.z + dz) % NZ
        return (y * NC + (self.c + dc) % NC, x * NZ + z)


def greet(others):
    barrier = pltpu.get_barrier_semaphore()
    for other in others:
        pl.semaphore_signal(barrier, inc=1, device_id=other, device_id_type=MESH)
    pl.semaphore_wait(barrier, len(others))


class Copies:
    def __init__(self, send, recv):
        self.send, self.recv, self.used, self.sent = send, recv, 0, []

    def start(self, src, dst, device):
        i = self.used
        self.used += 1
        copy = pltpu.make_async_remote_copy(
            src_ref=src, dst_ref=dst, send_sem=self.send.at[i], recv_sem=self.recv.at[i],
            device_id=device, device_id_type=MESH,
        )
        copy.start()
        self.sent.append(copy)
        return copy

    def finish(self):
        for copy in self.sent:
            copy.wait_send()


def dot(a, b, dims):
    return lax.dot_general(a, b, (dims, ((), ())), preferred_element_type=F32)


def sigmoid(v):
    return 1.0 / (1.0 + jnp.exp(-v))


def iota(shape, dim):
    return lax.broadcasted_iota(jnp.int32, shape, dim)


def kernel(
    enc, w, meta, bw_hbm, out_h, out_c, out_b,
    docs, docs_t, wrel, bw, metas, pos_t, arr, tgt, off, place, disp, rows_p, delta,
    ret, hid, zs_r, zs_l, zr_r, zr_l,
    gc, c_in, x_r2, x_l2, x_s, x_r, x_y, cy_2, cy_s, cy_r,
    gb, b_in, by_2, by_s, by_r, send, recv, local,
):
    me = Spot()
    x, y, z, c = me.x, me.y, me.z, me.c
    scale = 1.0 / math.sqrt(DOC * NY * NC * NX * NZ)
    own = [
        pltpu.make_async_copy(enc, docs.at[z], local.at[0]),
        pltpu.make_async_copy(meta, metas.at[z], local.at[1]),
        pltpu.make_async_copy(w, wrel.at[0], local.at[2]),
        pltpu.make_async_copy(bw_hbm, bw, local.at[3]),
    ]
    for copy in own:
        copy.start()
    greet(
        [me.at(dz=i) for i in range(1, NZ)] + [me.at(dx=i) for i in range(1, NX)]
        + [me.at(dy=1), me.at(dy=-1), me.at(dc=1)]
    )
    cp = Copies(send, recv)
    half = DOC // 2
    right = cp.start(enc, docs.at[z], me.at(dz=1))
    left = cp.start(enc, docs.at[z], me.at(dz=-1))
    got_meta = [None] + [cp.start(meta, metas.at[z], me.at(dz=i)) for i in range(1, NZ)]
    w_right = cp.start(w.at[y, c], wrel.at[3, y, c], me.at(dx=1))
    w_left = cp.start(w.at[y, c], wrel.at[1, y, c], me.at(dx=-1))

    slot = iota((128, 128), 0)
    lane = iota((128, 128), 1)
    block = (((x + (slot >> 5)) & 3) * NZ + z) * 16 + (slot & 15)
    turn = ((slot >> 4) & 1).astype(F32)
    upper = jnp.where(slot < lane, 1.0, 0.0).astype(BF16)
    eye = jnp.where(slot == lane, 1.0, 0.0).astype(BF16)
    row8 = iota((8, 128), 0)
    tgt[0] = jnp.zeros((8, 128), F32)
    arrivals = [[] for _ in range(NX)]

    def dispatch(zs):
        info = metas[zs]
        named = jnp.zeros((128, 128), F32)
        offset = jnp.zeros((128, 128), F32)
        for k in range(4):
            hit = info[4 + k:5 + k, :] == block
            named = jnp.where(hit, 1.0, named)
            offset = jnp.where(hit, (info[8 + k:9 + k, :] + 1).astype(F32), offset)
        rank = dot(named.astype(BF16), upper, ((1,), (0,)))
        chosen = jnp.where(rank == turn, named, 0.0)
        place[zs] = chosen.astype(BF16)
        disp[zs] = dot(chosen.astype(BF16), docs[zs], ((1,), (0,))).astype(BF16)
        for d in range(1, NX):
            arrivals[NX - d].append(
                cp.start(disp.at[zs, pl.ds(d * 32, 32)], arr.at[NX - d, zs], me.at(dx=d))
            )
        arr[0, zs] = disp[zs, 0:32]
        pick = jnp.where(row8 == zs, 1.0, 0.0).astype(BF16)
        tgt[0] += dot(pick, (chosen * offset).astype(BF16), ((1,), (1,)))

    def prepare(zs):
        columns = pl.ds(pl.multiple_of(zs * 128, 128), 128)
        for j in range(D // 128):
            docs_t[pl.ds(j * 128, 128), columns] = dot(
                eye, docs[zs, :, j * 128:(j + 1) * 128], ((1,), (1,))
            ).astype(BF16)
        pos_t[columns, :] = jnp.transpose(metas[zs].astype(F32), (1, 0))

    def first(tile, pos, base):
        ids = (base + iota((1, tile.shape[1]), 1)).astype(F32)
        hit = pos[:, 0:1] == ids
        for k in range(1, 4):
            hit = hit | (pos[:, k:k + 1] == ids)
        return (sigmoid(tile) - jnp.where(hit, 1.0, 0.0)).astype(BF16)

    def own_group(zs):
        rows = pl.ds(pl.multiple_of(zs * 128, 128), 128)
        tile = dot(docs[zs], wrel[0].reshape(CL, D), ((1,), (1,)))
        delta[rows, 0:CL] = first(tile, pos_t[rows, :], (x * NZ + z) * CL)

    own[0].wait()
    own[1].wait()
    dispatch(z)
    prepare(z)
    own[2].wait()
    own_group(z)
    groups = pl.ds(1, 3)
    for h in range(1, NZ // 2):
        from_left, from_right = (z - h) % NZ, (z + h) % NZ
        right.wait_recv()
        left.wait_recv()
        if h + 1 < NZ // 2:
            right = cp.start(docs.at[from_left], docs.at[from_left], me.at(dz=1))
            left = cp.start(docs.at[from_right], docs.at[from_right], me.at(dz=-1))
        else:
            right = cp.start(
                docs.at[from_left, pl.ds(0, half)], docs.at[from_left, pl.ds(0, half)], me.at(dz=1)
            )
            left = cp.start(
                docs.at[from_right, pl.ds(half, half)], docs.at[from_right, pl.ds(half, half)], me.at(dz=-1)
            )
        if h == 1:
            w_right.wait_recv()
            w_left.wait_recv()
            w_right = cp.start(w_part(wrel, 3, y, c, 0), w_part(wrel, 2, y, c, 0), me.at(dx=1))
            w_left = cp.start(w_part(wrel, 1, y, c, 1), w_part(wrel, 2, y, c, 1), me.at(dx=-1))
        if h == 2:
            w_right.wait_recv()
            w_left.wait_recv()
            y_right = cp.start(wrel.at[groups, y, c], wrel.at[groups, y, c], me.at(dy=1))
            y_left = cp.start(wrel.at[groups, y, c], wrel.at[groups, y, c], me.at(dy=-1))
            sib = [cp.start(wrel.at[groups, y, c], wrel.at[groups, y, c], me.at(dc=1))]
        if h == 3:
            y_right.wait_recv()
            y_left.wait_recv()
            yl, yr = (y - 1) % NY, (y + 1) % NY
            sib.append(cp.start(wrel.at[groups, yl, c], wrel.at[groups, yl, c], me.at(dc=1)))
            sib.append(cp.start(wrel.at[groups, yr, c], wrel.at[groups, yr, c], me.at(dc=1)))
            a, b = pl.ds(0, 32), pl.ds(32, 32)
            y_right = cp.start(wrel.at[groups, yl, c, a], wrel.at[groups, yl, c, a], me.at(dy=1))
            y_left = cp.start(wrel.at[groups, yr, c, b], wrel.at[groups, yr, c, b], me.at(dy=-1))
        got_meta[h].wait_recv()
        dispatch(from_left)
        got_meta[NZ - h].wait_recv()
        dispatch(from_right)
        for zs in (from_left, from_right):
            prepare(zs)
            own_group(zs)
    y_right.wait_recv()
    y_left.wait_recv()
    far = (y + 2) % NY
    sib.append(cp.start(wrel.at[groups, far, c], wrel.at[groups, far, c], me.at(dc=1)))
    right.wait_recv()
    left.wait_recv()
    got_meta[NZ // 2].wait_recv()
    opposite = (z + NZ // 2) % NZ
    dispatch(opposite)
    for d in range(1, NX):
        arrivals[NX - d].append(cp.start(tgt.at[0], tgt.at[NX - d], me.at(dx=d)))
    prepare(opposite)
    own_group(opposite)

    to, fro = iota((256, 256), 0), iota((256, 256), 1)
    moved = ((to >> 1) & 7) * 32 + (to & 1) * 16 + (to >> 4)
    shuffle = jnp.where(fro == moved, 1.0, 0.0).astype(BF16)
    offs = jnp.zeros((16, 64), F32)
    for e in range(NX):
        for copy in arrivals[e]:
            copy.wait_recv()
        rows = dot(shuffle, arr[e].reshape(256, D), ((1,), (0,))).astype(BF16)
        rows_p[:, e * 16:(e + 1) * 16, :] = rows.reshape(16, 16, D)
        for t in range(2):
            at = ((NX - e) % NX) * 32 + t * 16
            take = jnp.where(iota((16, 128), 1) == iota((16, 128), 0) + at, 1.0, 0.0).astype(BF16)
            put = jnp.where(iota((8, 64), 1) == iota((8, 64), 0) * 2 + (e * 16 + t), 1.0, 0.0).astype(BF16)
            taken = dot(take, tgt[e].astype(BF16), ((1,), (1,))).astype(BF16)
            offs = offs + dot(taken, put, ((1,), (0,)))
    off[...] = offs
    own[3].wait()

    def second(b, carry):
        rows, weight = rows_p[b], bw[b]
        scores = dot(weight, rows, ((1,), (1,)))
        wanted = off[pl.ds(b, 1), :]
        target = jnp.where(iota((LBL, 64), 0).astype(F32) + 1.0 == wanted, 1.0, 0.0)
        dt = jnp.where(wanted > 0.0, sigmoid(scores) - target, 0.0).astype(BF16)
        grad = dot(dt, rows, ((1,), (0,))) * scale
        at = pl.ds(pl.multiple_of(b * LBL, LBL), LBL)
        for j in range(NY * NC):
            gb[j // NC, j % NC, at, :] = grad[:, j * 128:(j + 1) * 128].astype(BF16)
        rows_p[b] = dot(dt, weight, ((0,), (0,))).astype(BF16)
        return carry

    lax.fori_loop(0, 16, second, 0)
    returns = []
    for e in (2, 1, 3, 0):
        rows = dot(shuffle, rows_p[:, e * 16:(e + 1) * 16, :].reshape(256, D), ((0,), (0,)))
        arr[e] = rows.astype(BF16).reshape(NZ, 32, D)
        if e > 0:
            dst = ret.at[pl.ds(0, NZ), pl.ds((NX - e) * 32, 32)]
            returns.append(cp.start(arr.at[e], dst, me.at(dx=e)))
        else:
            for i in range(NZ):
                ret[i, 0:32] = arr[0, i]
    b_core = cp.start(gb.at[pl.ds(0, NY), 1 - c], b_in, me.at(dc=1))

    for copy in sib:
        copy.wait_recv()

    def scores_one(t, carry):
        g, h = t // 2, t % 2
        weight = wrel[g, pl.ds(h * 2, 2)].reshape(256, D)
        tile = dot(docs[...].reshape(NZ * DOC, D), weight, ((1,), (1,)))
        base = (((x + g) % NX) * NZ + z) * CL + h * 256
        delta[:, pl.ds(pl.multiple_of(t * 256, 256), 256)] = first(tile, pos_t[...], base)
        return carry

    lax.fori_loop(2, 8, scores_one, 0)

    b_core.wait_recv()

    def add_block(i, carry):
        rows = pl.ds(pl.multiple_of((i % 4) * 512, 512), 512)
        gb[i // 4, c, rows] = (gb[i // 4, c, rows].astype(F32) + b_in[i // 4, rows].astype(F32)).astype(BF16)
        return carry

    lax.fori_loop(0, 16, add_block, 0)
    top, low = pl.ds(0, 1024), pl.ds(1024, 1024)
    b_right = cp.start(gb.at[far, c, top], by_2.at[top], me.at(dy=1))
    b_left = cp.start(gb.at[far, c, low], by_2.at[low], me.at(dy=-1))

    def grad_one(t, carry):
        columns = pl.ds(pl.multiple_of(t * 256, 256), 256)
        grad = dot(docs_t[...], delta[:, columns], ((1,), (0,))) * scale
        at = pl.ds(pl.multiple_of((t % 2) * 256, 256), 256)
        gc[:, :, t // 2, :, at] = grad.astype(BF16).reshape(NY, NC, 128, 256)
        return carry

    lax.fori_loop(0, 8, grad_one, 0)
    c_core = cp.start(gc.at[pl.ds(0, NY), 1 - c], c_in, me.at(dc=1))

    up, down = (y + 1) % NY, (y - 1) % NY
    b_right.wait_recv()
    b_left.wait_recv()

    def add_b(i, carry):
        rows = pl.ds(pl.multiple_of(i * 512, 512), 512)
        other = pl.ds(pl.multiple_of(i * 512 + 1024, 512), 512)
        by_s[0, rows] = (gb[up, c, rows].astype(F32) + by_2[rows].astype(F32)).astype(BF16)
        by_s[0, other] = gb[up, c, other]
        by_s[1, other] = (gb[down, c, other].astype(F32) + by_2[other].astype(F32)).astype(BF16)
        by_s[1, rows] = gb[down, c, rows]
        return carry

    lax.fori_loop(0, 2, add_b, 0)
    b_right = cp.start(by_s.at[0], by_r.at[0], me.at(dy=1))
    b_left = cp.start(by_s.at[1], by_r.at[1], me.at(dy=-1))

    def hidden_one(t, carry):
        columns = pl.ds(pl.multiple_of(t * 256, 256), 256)
        weight = wrel[:, :, :, :, columns].reshape(NX * CL, 256)
        hid[:, :, columns] = dot(delta[...], weight, ((1,), (0,))).reshape(NZ, DOC, 256)
        return carry

    lax.fori_loop(0, 4, hidden_one, 0)

    c_core.wait_recv()

    def add_cluster(i, carry):
        t, g = i // 4, i % 4
        gc[t, c, g] = (gc[t, c, g].astype(F32) + c_in[t, g].astype(F32)).astype(BF16)
        return carry

    lax.fori_loop(0, 16, add_cluster, 0)
    x_right = cp.start(gc.at[pl.ds(0, 2), c, 2], x_r2, me.at(dx=1))
    x_left = cp.start(gc.at[pl.ds(2, 2), c, 2], x_l2, me.at(dx=-1))

    for copy in returns:
        copy.wait_recv()

    def combine(t):
        hid[t] = hid[t] + dot(place[t], ret[t], ((0,), (0,)))

    combine(opposite)
    zs_r[3, 0:half] = hid[opposite, 0:half].astype(BF16)
    zs_l[3, half:DOC] = hid[opposite, half:DOC].astype(BF16)
    a, b = pl.ds(0, half), pl.ds(half, half)
    z_right = cp.start(zs_r.at[3, a], zr_r.at[3, a], me.at(dz=1))
    z_left = cp.start(zs_l.at[3, b], zr_l.at[3, b], me.at(dz=-1))

    def z_step(h):
        right, left = (z + h) % NZ, (z - h) % NZ
        combine(right)
        combine(left)
        z_right.wait_recv()
        z_left.wait_recv()
        if h == 3:
            zs_r[2, 0:half] = (hid[right, 0:half] + zr_r[3, 0:half].astype(F32)).astype(BF16)
            zs_r[2, half:DOC] = hid[right, half:DOC].astype(BF16)
            zs_l[2, half:DOC] = (hid[left, half:DOC] + zr_l[3, half:DOC].astype(F32)).astype(BF16)
            zs_l[2, 0:half] = hid[left, 0:half].astype(BF16)
        else:
            zs_r[h - 1] = (hid[right] + zr_r[h].astype(F32)).astype(BF16)
            zs_l[h - 1] = (hid[left] + zr_l[h].astype(F32)).astype(BF16)
        return (
            cp.start(zs_r.at[h - 1], zr_r.at[h - 1], me.at(dz=1)),
            cp.start(zs_l.at[h - 1], zr_l.at[h - 1], me.at(dz=-1)),
        )

    z_right, z_left = z_step(3)

    x_right.wait_recv()
    x_left.wait_recv()

    def add_x(i, carry):
        x_s[0, i] = (gc[i, c, 1].astype(F32) + x_r2[i].astype(F32)).astype(BF16)
        x_s[0, i + 2] = gc[i + 2, c, 1]
        x_s[1, i + 2] = (gc[i + 2, c, 3].astype(F32) + x_l2[i].astype(F32)).astype(BF16)
        x_s[1, i] = gc[i, c, 3]
        return carry

    lax.fori_loop(0, 2, add_x, 0)
    x_right = cp.start(x_s.at[0], x_r.at[0], me.at(dx=1))
    x_left = cp.start(x_s.at[1], x_r.at[1], me.at(dx=-1))

    z_right, z_left = z_step(2)

    x_right.wait_recv()
    x_left.wait_recv()

    def add_x2(i, carry):
        x_y[i] = (gc[i, c, 0].astype(F32) + x_r[0, i].astype(F32) + x_r[1, i].astype(F32)).astype(BF16)
        return carry

    lax.fori_loop(0, NY, add_x2, 0)
    ct, cl = pl.ds(0, 64), pl.ds(64, 64)
    c_right = cp.start(x_y.at[far, ct], cy_2.at[ct], me.at(dy=1))
    c_left = cp.start(x_y.at[far, cl], cy_2.at[cl], me.at(dy=-1))

    z_right, z_left = z_step(1)

    c_right.wait_recv()
    c_left.wait_recv()
    cy_s[0, ct] = (x_y[up, ct].astype(F32) + cy_2[ct].astype(F32)).astype(BF16)
    cy_s[0, cl] = x_y[up, cl]
    cy_s[1, cl] = (x_y[down, cl].astype(F32) + cy_2[cl].astype(F32)).astype(BF16)
    cy_s[1, ct] = x_y[down, ct]
    c_right = cp.start(cy_s.at[0], cy_r.at[0], me.at(dy=1))
    c_left = cp.start(cy_s.at[1], cy_r.at[1], me.at(dy=-1))

    combine(z)
    b_right.wait_recv()
    b_left.wait_recv()

    def add_b2(i, carry):
        rows = pl.ds(pl.multiple_of(i * 512, 512), 512)
        out_b[rows] = gb[y, c, rows].astype(F32) + by_r[0, rows].astype(F32) + by_r[1, rows].astype(F32)
        return carry

    lax.fori_loop(0, 4, add_b2, 0)
    z_right.wait_recv()
    z_left.wait_recv()
    out_h[...] = (hid[z] + zr_r[0].astype(F32) + zr_l[0].astype(F32)).astype(BF16)
    c_right.wait_recv()
    c_left.wait_recv()
    out_c[...] = x_y[y].astype(F32) + cy_r[0].astype(F32) + cy_r[1].astype(F32)
    cp.finish()


def w_part(wrel, group, y, c, part):
    return wrel.at[group, y, c, pl.ds(part * 32, 32)]


def per_device(encoded, positive_clusters, cluster_weight, shortlist, positive_offsets, block_weight):
    meta = jnp.concatenate(
        [positive_clusters.T, shortlist.T, positive_offsets.T, jnp.zeros((4, DOC), jnp.int32)], axis=0
    )
    vmem = pl.BlockSpec(memory_space=pltpu.VMEM)
    hbm = pl.BlockSpec(memory_space=pl.ANY)
    bf = lambda *shape: pltpu.VMEM(shape, BF16)
    f32 = lambda *shape: pltpu.VMEM(shape, F32)
    copies = 88
    out_h, out_c, out_b = pl.pallas_call(
        kernel,
        out_shape=(
            jax.ShapeDtypeStruct((DOC, D), BF16),
            jax.ShapeDtypeStruct((128, CL), F32),
            jax.ShapeDtypeStruct((2048, 128), F32),
        ),
        in_specs=[hbm] * 4,
        out_specs=(vmem,) * 3,
        scratch_shapes=[
            bf(NZ, DOC, D), bf(D, NZ * DOC), bf(NX, NY, NC, 64, D), bf(16, LBL, D),
            pltpu.VMEM((NZ, 16, 128), jnp.int32), f32(NZ * DOC, 16), bf(NX, NZ, 32, D), f32(NX, NZ, 128),
            f32(16, 64), bf(NZ, 128, 128), bf(NZ, 128, D), bf(16, 64, D), bf(NZ * DOC, NX * CL),
            bf(NZ, 128, D), f32(NZ, DOC, D), bf(4, DOC, D), bf(4, DOC, D), bf(4, DOC, D), bf(4, DOC, D),
            bf(NY, NC, NX, 128, CL), bf(NY, NX, 128, CL), bf(2, 128, CL), bf(2, 128, CL),
            bf(2, NY, 128, CL), bf(2, NY, 128, CL), bf(NY, 128, CL), bf(128, CL), bf(2, 128, CL), bf(2, 128, CL),
            bf(NY, NC, 2048, 128), bf(NY, 2048, 128), bf(2048, 128), bf(2, 2048, 128), bf(2, 2048, 128),
            pltpu.SemaphoreType.DMA((copies,)),
            pltpu.SemaphoreType.DMA((copies,)),
            pltpu.SemaphoreType.DMA((4,)),
        ],
        compiler_params=pltpu.CompilerParams(
            collective_id=0, has_side_effects=True, vmem_limit_bytes=VMEM_LIMIT
        ),
    )(encoded, cluster_weight.reshape(NY, NC, 64, D), meta, block_weight)
    return out_h, out_c.T, out_b.reshape(16, LBL, 128)


def solution(mesh):
    placed = (
        P(("dp", "label"), None),
        P(("dp", "label"), None),
        P("label", None),
        P(("dp", "label"), None),
        P(("dp", "label"), None),
        P("label", None, None),
    )
    return jax.shard_map(
        per_device,
        mesh=mesh,
        in_specs=placed,
        out_specs=(P(("dp", "label"), None), P("label", "dp"), P("label", None, "dp")),
        check_vma=False,
    )
```

time: 190 us -> 115 us (0.61)
  the two profiles are of different devices: /device:TPU:8 before, /device:TPU:18 now
where the time goes in v2:
time: 115 us
  Pallas kernels  107 us (93%)
  local copies, waits for them, and re-layouts  5.83 us (5%)
  other arithmetic  1.38 us (1%)
    pallas_call x1, Pallas kernels, per_device(): pl.pallas_call(kernel, out_shape=(jax.ShapeDtypeStruct((DOC, D), BF16), j...  107 us
    unnamed x3, local copies, waits for them, and re-layouts  5.75 us

profile of v2, /device:TPU:18, one launch (start us, length us, event | category | flops | bytes accessed | tf_op | source)
XLA Modules:
  0.0 115.2 jit_solution(10005200454757000031)
XLA Ops:
  0.6 0.1 pad.3.clone
  0.7 1.4 %add_add_fusion.meta = s32[16,128]{1,0:T(8,128)} fusion(s32[4,128]{1,0:T(4,128)} %bitcast.9, s32[4,128]{1,0:T(4,128)} %bitcast.10, s32[4,128]{1,0:T(4,128)} %bitcast.11, s32[16]{0:T(128)S(1)} %pad.3.clone), kind=kLoop, calls=%fused_computation | loop fusion | flops 6144 | bytes 14400 | tf_op jit(solution)/shard_map/concatenate | solution.py:421
  2.1 107.3 %shard_map.85 = (bf16[128,1024]{1,0:T(8,128)(2,1)}, f32[128,512]{1,0:T(8,128)}, f32[2048,128]{1,0:T(8,128)}) custom-call(bf16[128,1024]{1,0:T(8,128)(2,1)} %enc.1, bf16[4,2,64,1024]{3,2,1,0:T(8,128)(2,1)} %bitcast.7, s32[16,128]{1,0:T(8,128)} %add_add_fusion.meta, bf16[16,128,1024]{2,1,0:T(8,128)(2,1)} %bw_hbm.1), custom_call_target="tpu_custom_call" | custom-call | tf_op jit(solution)/shard_map/pallas_call | solution.py:429
  109.4 1.8 %copy.9 = f32[512,128]{1,0:T(8,128)} copy(f32[512,128]{0,1:T(8,128)} %bitcast.8) | data formatting | bytes 524288
  111.2 1.7 %copy.12 = bf16[128,1024]{1,0:T(8,128)(2,1)} copy(bf16[128,1024]{1,0:T(8,128)(2,1)} %get-tuple-element.15) | data formatting | bytes 524288
  112.9 2.3 %copy.13 = f32[16,128,128]{2,1,0:T(8,128)} copy(f32[16,128,128]{2,1,0:T(8,128)} %bitcast.6) | data formatting | bytes 2097152
  (1 shorter events, 0.0 us)

commit v3 on v2

v3 whole, which is shorter than its diff:
```python
import math

import jax
import jax.numpy as jnp
from jax import lax
from jax.experimental import pallas as pl
from jax.experimental.pallas import tpu as pltpu
from jax.sharding import PartitionSpec as P

MESH = pl.DeviceIdType.MESH
F32, BF16 = jnp.float32, jnp.bfloat16
NY, NC, NX, NZ = 4, 2, 4, 8
DOC, D, CL, LBL = 128, 1024, 512, 128
VMEM_LIMIT = 60 * 1024 * 1024


class Spot:
    def __init__(self):
        dp, label = lax.axis_index("dp"), lax.axis_index("label")
        self.y, self.c = dp // NC, dp % NC
        self.x, self.z = label // NZ, label % NZ

    def at(self, dx=0, dy=0, dz=0, dc=0):
        y, x, z = (self.y + dy) % NY, (self.x + dx) % NX, (self.z + dz) % NZ
        return (y * NC + (self.c + dc) % NC, x * NZ + z)


class Copies:
    def __init__(self, send, recv):
        self.send, self.recv, self.used, self.sent = send, recv, 0, []

    def start(self, src, dst, device):
        i = self.used
        self.used += 1
        copy = pltpu.make_async_remote_copy(
            src_ref=src, dst_ref=dst, send_sem=self.send.at[i], recv_sem=self.recv.at[i],
            device_id=device, device_id_type=MESH,
        )
        copy.start()
        self.sent.append(copy)
        return copy

    def finish(self):
        for copy in self.sent:
            copy.wait_send()


def dot(a, b, dims):
    return lax.dot_general(a, b, (dims, ((), ())), preferred_element_type=F32)


def sigmoid(v):
    return 1.0 / (1.0 + jnp.exp(-v))


def iota(shape, dim):
    return lax.broadcasted_iota(jnp.int32, shape, dim)


def kernel(
    enc, w, pos, listed, offsets, bw_hbm, out_h, out_c, out_b,
    docs, docs_t, wrel, bw, metas, pos_t, arr, tgt, off, place, disp, rows_p, delta,
    ret, hid, zs_r, zs_l, zr_r, zr_l,
    gc, c_in, cy_2, cy_s, cy_r, c_y, x_2, x_s, x_r,
    gb, b_in, by_2, by_s, by_r, o_h, o_c, o_b, send, recv, local,
):
    me = Spot()
    x, y, z, c = me.x, me.y, me.z, me.c
    scale = 1.0 / math.sqrt(DOC * NY * NC * NX * NZ)
    own = [
        pltpu.make_async_copy(enc, docs.at[z], local.at[0]),
        pltpu.make_async_copy(pos, metas.at[z, pl.ds(0, 4)], local.at[1]),
        pltpu.make_async_copy(listed, metas.at[z, pl.ds(4, 4)], local.at[2]),
        pltpu.make_async_copy(offsets, metas.at[z, pl.ds(8, 4)], local.at[3]),
        pltpu.make_async_copy(w, wrel.at[0], local.at[4]),
        pltpu.make_async_copy(bw_hbm, bw, local.at[5]),
    ]
    for copy in own:
        copy.start()
    metas[z, 12:16] = jnp.zeros((4, 128), jnp.int32)
    others = (
        [me.at(dz=i) for i in range(1, NZ)] + [me.at(dx=i) for i in range(1, NX)]
        + [me.at(dy=1), me.at(dy=-1), me.at(dc=1)]
    )
    barrier = pltpu.get_barrier_semaphore()
    for other in others:
        pl.semaphore_signal(barrier, inc=1, device_id=other, device_id_type=MESH)
    cp = Copies(send, recv)
    half = DOC // 2

    slot = iota((128, 128), 0)
    lane = iota((128, 128), 1)
    block = (((x + (slot >> 5)) & 3) * NZ + z) * 16 + (slot & 15)
    turn = ((slot >> 4) & 1).astype(F32)
    upper = jnp.where(slot < lane, 1.0, 0.0).astype(BF16)
    eye = jnp.where(slot == lane, 1.0, 0.0).astype(BF16)
    row8 = iota((8, 128), 0)
    tgt[0] = jnp.zeros((8, 128), F32)
    arrivals = [[] for _ in range(NX)]

    def choose(zs):
        info = metas[zs]
        named = jnp.zeros((128, 128), F32)
        offset = jnp.zeros((128, 128), F32)
        for k in range(4):
            hit = info[4 + k:5 + k, :] == block
            named = jnp.where(hit, 1.0, named)
            offset = jnp.where(hit, (info[8 + k:9 + k, :] + 1).astype(F32), offset)
        rank = dot(named.astype(BF16), upper, ((1,), (0,)))
        chosen = jnp.where(rank == turn, named, 0.0)
        place[zs] = chosen.astype(BF16)
        disp[zs] = dot(chosen.astype(BF16), docs[zs], ((1,), (0,))).astype(BF16)
        pick = jnp.where(row8 == zs, 1.0, 0.0).astype(BF16)
        tgt[0] += dot(pick, (chosen * offset).astype(BF16), ((1,), (1,)))

    def hand_on(zs):
        for d in (2, 1, 3):
            arrivals[NX - d].append(
                cp.start(disp.at[zs, pl.ds(d * 32, 32)], arr.at[NX - d, zs], me.at(dx=d))
            )
        arr[0, zs] = disp[zs, 0:32]

    def dispatch(zs):
        choose(zs)
        hand_on(zs)

    def prepare(zs):
        columns = pl.ds(pl.multiple_of(zs * 128, 128), 128)
        for j in range(D // 128):
            docs_t[pl.ds(j * 128, 128), columns] = dot(
                eye, docs[zs, :, j * 128:(j + 1) * 128], ((1,), (1,))
            ).astype(BF16)
        pos_t[columns, :] = jnp.transpose(metas[zs].astype(F32), (1, 0))

    def first(tile, pos, base):
        ids = (base + iota((1, tile.shape[1]), 1)).astype(F32)
        hit = pos[:, 0:1] == ids
        for k in range(1, 4):
            hit = hit | (pos[:, k:k + 1] == ids)
        return (sigmoid(tile) - jnp.where(hit, 1.0, 0.0)).astype(BF16)

    def own_group(zs):
        rows = pl.ds(pl.multiple_of(zs * 128, 128), 128)
        tile = dot(docs[zs], wrel[0].reshape(CL, D), ((1,), (1,)))
        delta[rows, 0:CL] = first(tile, pos_t[rows, :], (x * NZ + z) * CL)

    for i in range(4):
        own[i].wait()
    choose(z)
    prepare(z)
    pl.semaphore_wait(barrier, len(others))
    right = cp.start(docs.at[z], docs.at[z], me.at(dz=1))
    left = cp.start(docs.at[z], docs.at[z], me.at(dz=-1))
    w_right = cp.start(w.at[y, c], wrel.at[3, y, c], me.at(dx=1))
    w_left = cp.start(w.at[y, c], wrel.at[1, y, c], me.at(dx=-1))
    got_meta = [None] + [cp.start(metas.at[z], metas.at[z], me.at(dz=i)) for i in range(1, NZ)]
    hand_on(z)
    own[4].wait()
    own_group(z)
    groups = pl.ds(1, 3)
    w_right.wait_recv()
    w_left.wait_recv()
    w_right = cp.start(w_part(wrel, 3, y, c, 0), w_part(wrel, 2, y, c, 0), me.at(dx=1))
    w_left = cp.start(w_part(wrel, 1, y, c, 1), w_part(wrel, 2, y, c, 1), me.at(dx=-1))
    for h in range(1, NZ // 2):
        from_left, from_right = (z - h) % NZ, (z + h) % NZ
        right.wait_recv()
        left.wait_recv()
        if h + 1 < NZ // 2:
            right = cp.start(docs.at[from_left], docs.at[from_left], me.at(dz=1))
            left = cp.start(docs.at[from_right], docs.at[from_right], me.at(dz=-1))
        else:
            right = cp.start(
                docs.at[from_left, pl.ds(0, half)], docs.at[from_left, pl.ds(0, half)], me.at(dz=1)
            )
            left = cp.start(
                docs.at[from_right, pl.ds(half, half)], docs.at[from_right, pl.ds(half, half)], me.at(dz=-1)
            )
        if h == 1:
            w_right.wait_recv()
            w_left.wait_recv()
            y_right = cp.start(wrel.at[groups, y, c], wrel.at[groups, y, c], me.at(dy=1))
            y_left = cp.start(wrel.at[groups, y, c], wrel.at[groups, y, c], me.at(dy=-1))
            sib = [cp.start(wrel.at[groups, y, c], wrel.at[groups, y, c], me.at(dc=1))]
        got_meta[h].wait_recv()
        dispatch(from_left)
        got_meta[NZ - h].wait_recv()
        dispatch(from_right)
        for zs in (from_left, from_right):
            prepare(zs)
            own_group(zs)
        if h == 2:
            y_right.wait_recv()
            y_left.wait_recv()
            yl, yr = (y - 1) % NY, (y + 1) % NY
            a, b = pl.ds(0, 32), pl.ds(32, 32)
            y_right = cp.start(wrel.at[groups, yl, c, a], wrel.at[groups, yl, c, a], me.at(dy=1))
            y_left = cp.start(wrel.at[groups, yr, c, b], wrel.at[groups, yr, c, b], me.at(dy=-1))
            sib.append(cp.start(wrel.at[groups, yl, c], wrel.at[groups, yl, c], me.at(dc=1)))
            sib.append(cp.start(wrel.at[groups, yr, c], wrel.at[groups, yr, c], me.at(dc=1)))
        if h == 3:
            y_right.wait_recv()
            y_left.wait_recv()
            far = (y + 2) % NY
            sib.append(cp.start(wrel.at[groups, far, c], wrel.at[groups, far, c], me.at(dc=1)))
    right.wait_recv()
    left.wait_recv()
    got_meta[NZ // 2].wait_recv()
    opposite = (z + NZ // 2) % NZ
    dispatch(opposite)
    for d in range(1, NX):
        arrivals[NX - d].append(cp.start(tgt.at[0], tgt.at[NX - d], me.at(dx=d)))
    prepare(opposite)
    own_group(opposite)

    for copy in sib:
        copy.wait_recv()

    def scores_one(t, carry):
        g, h = t // 2, t % 2
        weight = wrel[g, pl.ds(h * 2, 2)].reshape(256, D)
        tile = dot(docs[...].reshape(NZ * DOC, D), weight, ((1,), (1,)))
        base = (((x + g) % NX) * NZ + z) * CL + h * 256
        delta[:, pl.ds(pl.multiple_of(t * 256, 256), 256)] = first(tile, pos_t[...], base)
        return carry

    lax.fori_loop(2, 8, scores_one, 0)

    def grad_one(t, carry):
        columns = pl.ds(pl.multiple_of(t * 256, 256), 256)
        grad = dot(docs_t[...], delta[:, columns], ((1,), (0,))) * scale
        at = pl.ds(pl.multiple_of((t % 2) * 256, 256), 256)
        gc[:, :, t // 2, :, at] = grad.astype(BF16).reshape(NY, NC, 128, 256)
        return carry

    c_core = []
    for g in range(NX):
        lax.fori_loop(2 * g, 2 * g + 2, grad_one, 0)
        c_core.append(
            cp.start(gc.at[pl.ds(0, NY), 1 - c, g], c_in.at[pl.ds(0, NY), g], me.at(dc=1))
        )


    to, fro = iota((256, 256), 0), iota((256, 256), 1)
    moved = ((to >> 1) & 7) * 32 + (to & 1) * 16 + (to >> 4)
    shuffle = jnp.where(fro == moved, 1.0, 0.0).astype(BF16)
    offs = jnp.zeros((16, 64), F32)
    for e in range(NX):
        for copy in arrivals[e]:
            copy.wait_recv()
        rows = dot(shuffle, arr[e].reshape(256, D), ((1,), (0,))).astype(BF16)
        rows_p[:, e * 16:(e + 1) * 16, :] = rows.reshape(16, 16, D)
        for t in range(2):
            at = ((NX - e) % NX) * 32 + t * 16
            take = jnp.where(iota((16, 128), 1) == iota((16, 128), 0) + at, 1.0, 0.0).astype(BF16)
            put = jnp.where(iota((8, 64), 1) == iota((8, 64), 0) * 2 + (e * 16 + t), 1.0, 0.0).astype(BF16)
            taken = dot(take, tgt[e].astype(BF16), ((1,), (1,))).astype(BF16)
            offs = offs + dot(taken, put, ((1,), (0,)))
    off[...] = offs
    own[5].wait()

    def second(b, carry):
        rows, weight = rows_p[b], bw[b]
        scores = dot(weight, rows, ((1,), (1,)))
        wanted = off[pl.ds(b, 1), :]
        target = jnp.where(iota((LBL, 64), 0).astype(F32) + 1.0 == wanted, 1.0, 0.0)
        dt = jnp.where(wanted > 0.0, sigmoid(scores) - target, 0.0).astype(BF16)
        grad = dot(dt, rows, ((1,), (0,))) * scale
        at = pl.ds(pl.multiple_of(b * LBL, LBL), LBL)
        for j in range(NY * NC):
            gb[j // NC, j % NC, at, :] = grad[:, j * 128:(j + 1) * 128].astype(BF16)
        rows_p[b] = dot(dt, weight, ((0,), (0,))).astype(BF16)
        return carry

    lax.fori_loop(0, 4, second, 0)

    up, down = (y + 1) % NY, (y - 1) % NY
    for copy in c_core:
        copy.wait_recv()

    def add_cluster(i, carry):
        t, g = i // 4, i % 4
        gc[t, c, g] = (gc[t, c, g].astype(F32) + c_in[t, g].astype(F32)).astype(BF16)
        return carry

    lax.fori_loop(0, 16, add_cluster, 0)
    first_two, last_two = pl.ds(0, 2), pl.ds(2, 2)
    c_right = cp.start(gc.at[far, c, first_two], cy_2.at[first_two], me.at(dy=1))
    c_left = cp.start(gc.at[far, c, last_two], cy_2.at[last_two], me.at(dy=-1))

    lax.fori_loop(4, 13, second, 0)
    c_right.wait_recv()
    c_left.wait_recv()

    def add_c(i, carry):
        cy_s[0, i] = (gc[up, c, i].astype(F32) + cy_2[i].astype(F32)).astype(BF16)
        cy_s[0, i + 2] = gc[up, c, i + 2]
        cy_s[1, i + 2] = (gc[down, c, i + 2].astype(F32) + cy_2[i + 2].astype(F32)).astype(BF16)
        cy_s[1, i] = gc[down, c, i]
        return carry

    lax.fori_loop(0, 2, add_c, 0)
    c_right = cp.start(cy_s.at[0], cy_r.at[0], me.at(dy=1))
    c_left = cp.start(cy_s.at[1], cy_r.at[1], me.at(dy=-1))

    lax.fori_loop(13, 16, second, 0)
    b_core = cp.start(gb.at[pl.ds(0, NY), 1 - c], b_in, me.at(dc=1))
    for e in (2, 1, 3, 0):
        rows = dot(shuffle, rows_p[:, e * 16:(e + 1) * 16, :].reshape(256, D), ((0,), (0,)))
        arr[e] = rows.astype(BF16).reshape(NZ, 32, D)
    returns = [[] for _ in range(NZ)]
    for i in (4, 3, -3, 2, -2, 1, -1, 0):
        t = (z + i) % NZ
        for e in (2, 1, 3):
            dst = ret.at[t, pl.ds((NX - e) * 32, 32)]
            returns[i % NZ].append(cp.start(arr.at[e, t], dst, me.at(dx=e)))
    for i in range(NZ):
        ret[i, 0:32] = arr[0, i]

    def hidden_one(t, carry):
        columns = pl.ds(pl.multiple_of(t * 256, 256), 256)
        weight = wrel[:, :, :, :, columns].reshape(NX * CL, 256)
        hid[:, :, columns] = dot(delta[...], weight, ((1,), (0,))).reshape(NZ, DOC, 256)
        return carry

    lax.fori_loop(0, 4, hidden_one, 0)

    def combine(i):
        t = (z + i) % NZ
        for copy in returns[i % NZ]:
            copy.wait_recv()
        hid[t] = hid[t] + dot(place[t], ret[t], ((0,), (0,)))

    def z_step(h):
        right, left = (z + h) % NZ, (z - h) % NZ
        combine(h)
        combine(-h)
        z_right.wait_recv()
        z_left.wait_recv()
        if h == 3:
            zs_r[2, 0:half] = (hid[right, 0:half] + zr_r[3, 0:half].astype(F32)).astype(BF16)
            zs_r[2, half:DOC] = hid[right, half:DOC].astype(BF16)
            zs_l[2, half:DOC] = (hid[left, half:DOC] + zr_l[3, half:DOC].astype(F32)).astype(BF16)
            zs_l[2, 0:half] = hid[left, 0:half].astype(BF16)
        else:
            zs_r[h - 1] = (hid[right] + zr_r[h].astype(F32)).astype(BF16)
            zs_l[h - 1] = (hid[left] + zr_l[h].astype(F32)).astype(BF16)
        return (
            cp.start(zs_r.at[h - 1], zr_r.at[h - 1], me.at(dz=1)),
            cp.start(zs_l.at[h - 1], zr_l.at[h - 1], me.at(dz=-1)),
        )

    combine(4)
    zs_r[3, 0:half] = hid[opposite, 0:half].astype(BF16)
    zs_l[3, half:DOC] = hid[opposite, half:DOC].astype(BF16)
    a, b = pl.ds(0, half), pl.ds(half, half)
    z_right = cp.start(zs_r.at[3, a], zr_r.at[3, a], me.at(dz=1))
    z_left = cp.start(zs_l.at[3, b], zr_l.at[3, b], me.at(dz=-1))

    b_core.wait_recv()

    def add_block(i, carry):
        rows = pl.ds(pl.multiple_of((i % 4) * 512, 512), 512)
        gb[i // 4, c, rows] = (gb[i // 4, c, rows].astype(F32) + b_in[i // 4, rows].astype(F32)).astype(BF16)
        return carry

    lax.fori_loop(0, 16, add_block, 0)
    top, low = pl.ds(0, 1024), pl.ds(1024, 1024)
    b_right = cp.start(gb.at[far, c, top], by_2.at[top], me.at(dy=1))
    b_left = cp.start(gb.at[far, c, low], by_2.at[low], me.at(dy=-1))

    z_right, z_left = z_step(3)

    c_right.wait_recv()
    c_left.wait_recv()

    def add_c2(i, carry):
        c_y[i] = (gc[y, c, i].astype(F32) + cy_r[0, i].astype(F32) + cy_r[1, i].astype(F32)).astype(BF16)
        return carry

    lax.fori_loop(0, NX, add_c2, 0)
    ct, cl = pl.ds(0, 64), pl.ds(64, 64)
    x_right = cp.start(c_y.at[2, ct], x_2.at[ct], me.at(dx=1))
    x_left = cp.start(c_y.at[2, cl], x_2.at[cl], me.at(dx=-1))

    z_right, z_left = z_step(2)

    b_right.wait_recv()
    b_left.wait_recv()

    def add_b(i, carry):
        rows = pl.ds(pl.multiple_of(i * 512, 512), 512)
        other = pl.ds(pl.multiple_of(i * 512 + 1024, 512), 512)
        by_s[0, rows] = (gb[up, c, rows].astype(F32) + by_2[rows].astype(F32)).astype(BF16)
        by_s[0, other] = gb[up, c, other]
        by_s[1, other] = (gb[down, c, other].astype(F32) + by_2[other].astype(F32)).astype(BF16)
        by_s[1, rows] = gb[down, c, rows]
        return carry

    lax.fori_loop(0, 2, add_b, 0)
    b_right = cp.start(by_s.at[0], by_r.at[0], me.at(dy=1))
    b_left = cp.start(by_s.at[1], by_r.at[1], me.at(dy=-1))

    z_right, z_left = z_step(1)

    x_right.wait_recv()
    x_left.wait_recv()
    x_s[0, ct] = (c_y[1, ct].astype(F32) + x_2[ct].astype(F32)).astype(BF16)
    x_s[0, cl] = c_y[1, cl]
    x_s[1, cl] = (c_y[3, cl].astype(F32) + x_2[cl].astype(F32)).astype(BF16)
    x_s[1, ct] = c_y[3, ct]
    x_right = cp.start(x_s.at[0], x_r.at[0], me.at(dx=1))
    x_left = cp.start(x_s.at[1], x_r.at[1], me.at(dx=-1))

    combine(0)
    x_right.wait_recv()
    x_left.wait_recv()
    o_c[...] = c_y[0].astype(F32) + x_r[0].astype(F32) + x_r[1].astype(F32)
    done_c = pltpu.make_async_copy(o_c, out_c, local.at[6])
    done_c.start()
    b_right.wait_recv()
    b_left.wait_recv()

    def add_b2(i, carry):
        rows = pl.ds(pl.multiple_of(i * 512, 512), 512)
        o_b[rows] = gb[y, c, rows].astype(F32) + by_r[0, rows].astype(F32) + by_r[1, rows].astype(F32)
        return carry

    lax.fori_loop(0, 4, add_b2, 0)
    done_b = pltpu.make_async_copy(o_b, out_b, local.at[7])
    done_b.start()
    z_right.wait_recv()
    z_left.wait_recv()
    o_h[...] = (hid[z] + zr_r[0].astype(F32) + zr_l[0].astype(F32)).astype(BF16)
    done_h = pltpu.make_async_copy(o_h, out_h, local.at[8])
    done_h.start()
    for copy in (done_c, done_b, done_h):
        copy.wait()
    cp.finish()


def w_part(wrel, group, y, c, part):
    return wrel.at[group, y, c, pl.ds(part * 32, 32)]


def per_device(encoded, positive_clusters, cluster_weight, shortlist, positive_offsets, block_weight):
    vmem = pl.BlockSpec(memory_space=pltpu.VMEM)
    hbm = pl.BlockSpec(memory_space=pl.ANY)
    bf = lambda *shape: pltpu.VMEM(shape, BF16)
    f32 = lambda *shape: pltpu.VMEM(shape, F32)
    copies = 112
    out_h, out_c, out_b = pl.pallas_call(
        kernel,
        out_shape=(
            jax.ShapeDtypeStruct((DOC, D), BF16),
            jax.ShapeDtypeStruct((128, CL), F32),
            jax.ShapeDtypeStruct((2048, 128), F32),
        ),
        in_specs=[hbm] * 6,
        out_specs=(hbm,) * 3,
        scratch_shapes=[
            bf(NZ, DOC, D), bf(D, NZ * DOC), bf(NX, NY, NC, 64, D), bf(16, LBL, D),
            pltpu.VMEM((NZ, 16, 128), jnp.int32), f32(NZ * DOC, 16), bf(NX, NZ, 32, D), f32(NX, NZ, 128),
            f32(16, 64), bf(NZ, 128, 128), bf(NZ, 128, D), bf(16, 64, D), bf(NZ * DOC, NX * CL),
            bf(NZ, 128, D), f32(NZ, DOC, D), bf(4, DOC, D), bf(4, DOC, D), bf(4, DOC, D), bf(4, DOC, D),
            bf(NY, NC, NX, 128, CL), bf(NY, NX, 128, CL), bf(NX, 128, CL), bf(2, NX, 128, CL), bf(2, NX, 128, CL),
            bf(NX, 128, CL), bf(128, CL), bf(2, 128, CL), bf(2, 128, CL),
            bf(NY, NC, 2048, 128), bf(NY, 2048, 128), bf(2048, 128), bf(2, 2048, 128), bf(2, 2048, 128),
            bf(DOC, D), f32(128, CL), f32(2048, 128),
            pltpu.SemaphoreType.DMA((copies,)),
            pltpu.SemaphoreType.DMA((copies,)),
            pltpu.SemaphoreType.DMA((9,)),
        ],
        compiler_params=pltpu.CompilerParams(
            collective_id=0, has_side_effects=True, vmem_limit_bytes=VMEM_LIMIT
        ),
    )(
        encoded, cluster_weight.reshape(NY, NC, 64, D), positive_clusters.T, shortlist.T,
        positive_offsets.T, block_weight,
    )
    out_h, out_c, out_b = pl.pallas_call(
        place_kernel,
        out_shape=(
            jax.ShapeDtypeStruct((DOC, D), BF16),
            jax.ShapeDtypeStruct((CL, 128), F32),
            jax.ShapeDtypeStruct((2048, 128), F32),
        ),
        in_specs=[vmem] * 3,
        out_specs=(vmem,) * 3,
    )(out_h, out_c, out_b)
    return out_h, out_c, out_b.reshape(16, LBL, 128)


def place_kernel(in_h, in_c, in_b, out_h, out_c, out_b):
    out_h[...] = in_h[...]
    out_c[...] = jnp.transpose(in_c[...], (1, 0))
    out_b[...] = in_b[...]


def solution(mesh):
    placed = (
        P(("dp", "label"), None),
        P(("dp", "label"), None),
        P("label", None),
        P(("dp", "label"), None),
        P(("dp", "label"), None),
        P("label", None, None),
    )
    return jax.shard_map(
        per_device,
        mesh=mesh,
        in_specs=placed,
        out_specs=(P(("dp", "label"), None), P("label", "dp"), P("label", None, "dp")),
        check_vma=False,
    )
```

time: 115 us -> 102 us (0.89)
  the two profiles are of different devices: /device:TPU:18 before, /device:TPU:2 now
where the time goes in v3:
time: 102 us
  Pallas kernels  101 us (99%)
    pallas_call x1, Pallas kernels, per_device(): pl.pallas_call(kernel, out_shape=(jax.ShapeDtypeStruct((DOC, D), BF16), j...  98.7 us
    pallas_call x1, Pallas kernels, per_device(): pl.pallas_call(place_kernel, out_shape=(jax.ShapeDtypeStruct((DOC, D), BF...  2.61 us

profile of v3, /device:TPU:2, one launch (start us, length us, event | category | flops | bytes accessed | tf_op | source)
XLA Modules:
  0.0 102.0 jit_solution(12734014033657181856)
XLA Ops:
  0.6 98.7 %shard_map.85 = (bf16[128,1024]{1,0:T(8,128)(2,1)}, f32[128,512]{1,0:T(8,128)}, f32[2048,128]{1,0:T(8,128)}) custom-call(bf16[128,1024]{1,0:T(8,128)(2,1)} %enc.1, bf16[4,2,64,1024]{3,2,1,0:T(8,128)(2,1)} %bitcast.5, s32[4,128]{1,0:T(4,128)} %bitcast.6, s32[4,128]{1,0:T(4,128)} %bitcast.7, s32[4,128]{1,0:T(4,128)} %bitcast.8, bf16[16,128,1024]{2,1,0:T(8,128)(2,1)} %bw_hbm.1), custom_call_target="tpu_custom_call" | custom-call | tf_op jit(solution)/shard_map/pallas_call | solution.py:452
  99.4 2.6 %shard_map.86 = (bf16[128,1024]{1,0:T(8,128)(2,1)}, f32[512,128]{1,0:T(8,128)}, f32[2048,128]{1,0:T(8,128)}) custom-call(bf16[128,1024]{1,0:T(8,128)(2,1)} %get-tuple-element.9.in_h, f32[128,512]{1,0:T(8,128)} %get-tuple-element.10.in_c, f32[2048,128]{1,0:T(8,128)} %get-tuple-element.11.in_b), custom_call_target="tpu_custom_call" | custom-call | tf_op jit(solution)/shard_map/pallas_call | solution.py:481

commit v4 on v3

v4 whole, which is shorter than its diff:
```python
import math

import jax
import jax.numpy as jnp
from jax import lax
from jax.experimental import pallas as pl
from jax.experimental.pallas import tpu as pltpu
from jax.sharding import PartitionSpec as P

MESH = pl.DeviceIdType.MESH
F32, BF16 = jnp.float32, jnp.bfloat16
NY, NC, NX, NZ = 4, 2, 4, 8
DOC, D, CL, LBL = 128, 1024, 512, 128
VMEM_LIMIT = 60 * 1024 * 1024


class Spot:
    def __init__(self):
        dp, label = lax.axis_index("dp"), lax.axis_index("label")
        self.y, self.c = dp // NC, dp % NC
        self.x, self.z = label // NZ, label % NZ

    def at(self, dx=0, dy=0, dz=0, dc=0):
        y, x, z = (self.y + dy) % NY, (self.x + dx) % NX, (self.z + dz) % NZ
        return (y * NC + (self.c + dc) % NC, x * NZ + z)


class Copies:
    def __init__(self, send, recv):
        self.send, self.recv, self.used, self.sent = send, recv, 0, []

    def start(self, src, dst, device):
        i = self.used
        self.used += 1
        copy = pltpu.make_async_remote_copy(
            src_ref=src, dst_ref=dst, send_sem=self.send.at[i], recv_sem=self.recv.at[i],
            device_id=device, device_id_type=MESH,
        )
        copy.start()
        self.sent.append(copy)
        return copy

    def finish(self):
        for copy in self.sent:
            copy.wait_send()


class Chain:
    def __init__(self, cp, side, own, two, s, r, rows=0):
        self.cp, self.side, self.own, self.two, self.s, self.r, self.rows = cp, side, own, two, s, r, rows

    def piece(self, j):
        return pl.ds(j * self.rows, self.rows) if self.rows else j

    def pair(self, j):
        return pl.ds(j * (self.rows or 1), 2 * (self.rows or 1))

    def begin(self):
        a, b = self.pair(0), self.pair(2)
        self.moving = [
            self.cp.start(self.own(2, a), self.two.at[a], self.side(1)),
            self.cp.start(self.own(2, b), self.two.at[b], self.side(-1)),
        ]

    def arrive(self):
        for copy in self.moving:
            copy.wait_recv()

    def middle(self):
        self.arrive()
        for j in range(4):
            at = self.piece(j)
            self.s[j // 2, at] = (self.own(1 + j // 2 * 2, at)[...].astype(F32) + self.two[at].astype(F32)).astype(BF16)
            self.s[1 - j // 2, at] = self.own(3 - j // 2 * 2, at)[...]
        self.moving = [
            self.cp.start(self.s.at[0], self.r.at[0], self.side(1)),
            self.cp.start(self.s.at[1], self.r.at[1], self.side(-1)),
        ]

    def end(self, put):
        self.arrive()
        for j in range(4):
            at = self.piece(j)
            put(at, self.own(0, at)[...].astype(F32) + self.r[0, at].astype(F32) + self.r[1, at].astype(F32))


def dot(a, b, dims):
    return lax.dot_general(a, b, (dims, ((), ())), preferred_element_type=F32)


def sigmoid(v):
    return 0.5 * jnp.tanh(0.5 * v) + 0.5


def iota(shape, dim):
    return lax.broadcasted_iota(jnp.int32, shape, dim)


def kernel(
    enc, w, pos, listed, offsets, bw_hbm, out_h, out_c, out_b,
    docs, docs_t, wrel, bw, metas, pos_t, arr, tgt, off, place, disp, rows_p, delta,
    ret, hid, zs_r, zs_l, zr_r, zr_l,
    gc, c_in, fa_2, fa_s, fa_r, fb_2, fb_s, fb_r, c_a, c_b, ga_2, ga_s, ga_r, gb_2, gb_s, gb_r,
    gb, b_in, by_2, by_s, by_r, o_h, o_c, o_b, send, recv, local,
):
    me = Spot()
    x, y, z, c = me.x, me.y, me.z, me.c
    scale = 1.0 / math.sqrt(DOC * NY * NC * NX * NZ)
    own = [
        pltpu.make_async_copy(enc, docs.at[z], local.at[0]),
        pltpu.make_async_copy(pos, metas.at[z, pl.ds(0, 4)], local.at[1]),
        pltpu.make_async_copy(listed, metas.at[z, pl.ds(4, 4)], local.at[2]),
        pltpu.make_async_copy(offsets, metas.at[z, pl.ds(8, 4)], local.at[3]),
        pltpu.make_async_copy(w, wrel.at[0], local.at[4]),
        pltpu.make_async_copy(bw_hbm, bw, local.at[5]),
    ]
    for copy in own:
        copy.start()
    metas[z, 12:16] = jnp.zeros((4, 128), jnp.int32)
    others = (
        [me.at(dz=i) for i in range(1, NZ)] + [me.at(dx=i) for i in range(1, NX)]
        + [me.at(dy=1), me.at(dy=-1), me.at(dc=1)]
    )
    barrier = pltpu.get_barrier_semaphore()
    for other in others:
        pl.semaphore_signal(barrier, inc=1, device_id=other, device_id_type=MESH)
    cp = Copies(send, recv)
    half = DOC // 2

    slot = iota((128, 128), 0)
    lane = iota((128, 128), 1)
    block = (((x + (slot >> 5)) & 3) * NZ + z) * 16 + (slot & 15)
    turn = ((slot >> 4) & 1).astype(F32)
    upper = jnp.where(slot < lane, 1.0, 0.0).astype(BF16)
    eye = jnp.where(slot == lane, 1.0, 0.0).astype(BF16)
    row8 = iota((8, 128), 0)
    tgt[0] = jnp.zeros((8, 128), F32)
    arrivals = [[] for _ in range(NX)]

    def choose(zs):
        info = metas[zs]
        named = jnp.zeros((128, 128), F32)
        offset = jnp.zeros((128, 128), F32)
        for k in range(4):
            hit = info[4 + k:5 + k, :] == block
            named = jnp.where(hit, 1.0, named)
            offset = jnp.where(hit, (info[8 + k:9 + k, :] + 1).astype(F32), offset)
        rank = dot(named.astype(BF16), upper, ((1,), (0,)))
        chosen = jnp.where(rank == turn, named, 0.0)
        place[zs] = chosen.astype(BF16)
        disp[zs] = dot(chosen.astype(BF16), docs[zs], ((1,), (0,))).astype(BF16)
        pick = jnp.where(row8 == zs, 1.0, 0.0).astype(BF16)
        tgt[0] += dot(pick, (chosen * offset).astype(BF16), ((1,), (1,)))

    def hand_on(zs):
        for d in (2, 1, 3):
            arrivals[NX - d].append(
                cp.start(disp.at[zs, pl.ds(d * 32, 32)], arr.at[NX - d, zs], me.at(dx=d))
            )
        arr[0, zs] = disp[zs, 0:32]

    def dispatch(zs):
        choose(zs)
        hand_on(zs)

    def prepare(zs):
        columns = pl.ds(pl.multiple_of(zs * 128, 128), 128)
        for j in range(D // 128):
            docs_t[pl.ds(j * 128, 128), columns] = dot(
                eye, docs[zs, :, j * 128:(j + 1) * 128], ((1,), (1,))
            ).astype(BF16)
        pos_t[columns, :] = jnp.transpose(metas[zs].astype(F32), (1, 0))

    def first(tile, pos, base):
        ids = (base + iota((1, tile.shape[1]), 1)).astype(F32)
        hit = pos[:, 0:1] == ids
        for k in range(1, 4):
            hit = hit | (pos[:, k:k + 1] == ids)
        return (sigmoid(tile) - jnp.where(hit, 1.0, 0.0)).astype(BF16)

    def own_group(zs):
        rows = pl.ds(pl.multiple_of(zs * 128, 128), 128)
        tile = dot(docs[zs], wrel[0].reshape(CL, D), ((1,), (1,)))
        delta[rows, 0:CL] = first(tile, pos_t[rows, :], (x * NZ + z) * CL)

    for i in range(4):
        own[i].wait()
    choose(z)
    prepare(z)
    pl.semaphore_wait(barrier, len(others))
    halves = (pl.ds(0, half), pl.ds(half, half))

    def pass_on(zs, part, dz):
        return cp.start(docs.at[zs, halves[part]], docs.at[zs, halves[part]], me.at(dz=dz))

    right, left = [None, None], [None, None]
    for part in range(2):
        right[part] = pass_on(z, part, 1)
        left[1 - part] = pass_on(z, 1 - part, -1)
    w_right = cp.start(w.at[y, c], wrel.at[3, y, c], me.at(dx=1))
    w_left = cp.start(w.at[y, c], wrel.at[1, y, c], me.at(dx=-1))
    got_meta = [None] + [cp.start(metas.at[z], metas.at[z], me.at(dz=i)) for i in range(1, NZ)]
    own[4].wait()
    own_group(z)
    groups = pl.ds(1, 3)
    w_right.wait_recv()
    w_left.wait_recv()
    w_right = cp.start(w_part(wrel, 3, y, c, 0), w_part(wrel, 2, y, c, 0), me.at(dx=1))
    w_left = cp.start(w_part(wrel, 1, y, c, 1), w_part(wrel, 2, y, c, 1), me.at(dx=-1))
    hand_on(z)
    for h in range(1, NZ // 2):
        from_left, from_right = (z - h) % NZ, (z + h) % NZ
        for part in range(2):
            right[part].wait_recv()
            if h + 1 < NZ // 2 or part == 0:
                right[part] = pass_on(from_left, part, 1)
            left[1 - part].wait_recv()
            if h + 1 < NZ // 2 or part == 0:
                left[1 - part] = pass_on(from_right, 1 - part, -1)
        if h == 1:
            w_right.wait_recv()
            w_left.wait_recv()
            y_right = cp.start(wrel.at[groups, y, c], wrel.at[groups, y, c], me.at(dy=1))
            y_left = cp.start(wrel.at[groups, y, c], wrel.at[groups, y, c], me.at(dy=-1))
            sib = [cp.start(wrel.at[groups, y, c], wrel.at[groups, y, c], me.at(dc=1))]
        got_meta[h].wait_recv()
        dispatch(from_left)
        got_meta[NZ - h].wait_recv()
        dispatch(from_right)
        if h == 3:
            y_right.wait_recv()
            y_left.wait_recv()
            yl, yr = (y - 1) % NY, (y + 1) % NY
            a, b = pl.ds(0, 32), pl.ds(32, 32)
            y_right = cp.start(wrel.at[groups, yl, c, a], wrel.at[groups, yl, c, a], me.at(dy=1))
            y_left = cp.start(wrel.at[groups, yr, c, b], wrel.at[groups, yr, c, b], me.at(dy=-1))
            sib.append(cp.start(wrel.at[groups, yl, c], wrel.at[groups, yl, c], me.at(dc=1)))
            sib.append(cp.start(wrel.at[groups, yr, c], wrel.at[groups, yr, c], me.at(dc=1)))
        for zs in (from_left, from_right):
            prepare(zs)
            own_group(zs)
    right[0].wait_recv()
    left[1].wait_recv()
    got_meta[NZ // 2].wait_recv()
    opposite = (z + NZ // 2) % NZ
    dispatch(opposite)
    for d in range(1, NX):
        arrivals[NX - d].append(cp.start(tgt.at[0], tgt.at[NX - d], me.at(dx=d)))
    prepare(opposite)
    own_group(opposite)

    def scores_one(copies, yi):
        for copy in copies:
            copy.wait_recv()
        weight = wrel[1:NX, yi].reshape(3 * 128, D)
        tile = dot(docs[...].reshape(NZ * DOC, D), weight, ((1,), (1,)))
        for g in range(1, NX):
            base = (((x + g) % NX) * NZ + z) * CL + yi * 128
            columns = pl.ds(pl.multiple_of(g * CL + yi * 128, 128), 128)
            delta[:, columns] = first(tile[:, (g - 1) * 128:g * 128], pos_t[...], base)

    scores_one(sib[0:1], y)
    scores_one(sib[1:2], yl)
    y_right.wait_recv()
    y_left.wait_recv()
    far = (y + 2) % NY
    sib.append(cp.start(wrel.at[groups, far, c], wrel.at[groups, far, c], me.at(dc=1)))
    scores_one(sib[2:3], yr)

    to, fro = iota((256, 256), 0), iota((256, 256), 1)
    moved = ((to >> 1) & 7) * 32 + (to & 1) * 16 + (to >> 4)
    shuffle = jnp.where(fro == moved, 1.0, 0.0).astype(BF16)
    offs = jnp.zeros((16, 64), F32)
    for e in range(NX):
        for copy in arrivals[e]:
            copy.wait_recv()
        rows = dot(shuffle, arr[e].reshape(256, D), ((1,), (0,))).astype(BF16)
        rows_p[:, e * 16:(e + 1) * 16, :] = rows.reshape(16, 16, D)
        for t in range(2):
            at = ((NX - e) % NX) * 32 + t * 16
            take = jnp.where(iota((16, 128), 1) == iota((16, 128), 0) + at, 1.0, 0.0).astype(BF16)
            put = jnp.where(iota((8, 64), 1) == iota((8, 64), 0) * 2 + (e * 16 + t), 1.0, 0.0).astype(BF16)
            taken = dot(take, tgt[e].astype(BF16), ((1,), (1,))).astype(BF16)
            offs = offs + dot(taken, put, ((1,), (0,)))
    off[...] = offs
    own[5].wait()

    def second(i, carry):
        pair = (2 * i, 2 * i + 1)
        scores = [dot(bw[b], rows_p[b], ((1,), (1,))) for b in pair]
        dts = []
        for b, score in zip(pair, scores):
            wanted = off[pl.ds(b, 1), :]
            target = jnp.where(iota((LBL, 64), 0).astype(F32) + 1.0 == wanted, 1.0, 0.0)
            dts.append(jnp.where(wanted > 0.0, sigmoid(score) - target, 0.0).astype(BF16))
        grads = [dot(dt, rows_p[b], ((1,), (0,))) for b, dt in zip(pair, dts)]
        backs = [dot(dt, bw[b], ((0,), (0,))) for b, dt in zip(pair, dts)]
        for b, grad, value in zip(pair, grads, backs):
            at = pl.ds(pl.multiple_of(b * LBL, LBL), LBL)
            grad = (grad * scale).astype(BF16)
            for j in range(NY * NC):
                gb[j // NC, j % NC, at, :] = grad[:, j * 128:(j + 1) * 128]
            rows_p[b] = value.astype(BF16)
        return carry

    b_core = []
    for i in range(2):
        lax.fori_loop(4 * i, 4 * i + 4, second, 0)
        rows = pl.ds(1024 * i, 1024)
        b_core.append(
            cp.start(gb.at[pl.ds(0, NY), 1 - c, rows], b_in.at[pl.ds(0, NY), rows], me.at(dc=1))
        )
    for e in (2, 1, 3, 0):
        rows = dot(shuffle, rows_p[:, e * 16:(e + 1) * 16, :].reshape(256, D), ((0,), (0,)))
        arr[e] = rows.astype(BF16).reshape(NZ, 32, D)
    returns = [[] for _ in range(NZ)]
    for i in (4, 3, -3, 2, -2, 1, -1, 0):
        t = (z + i) % NZ
        for e in (2, 1, 3):
            dst = ret.at[t, pl.ds((NX - e) * 32, 32)]
            returns[i % NZ].append(cp.start(arr.at[e, t], dst, me.at(dx=e)))
    for i in range(NZ):
        ret[i, 0:32] = arr[0, i]

    def grad_one(t, carry):
        columns = pl.ds(pl.multiple_of(t * 256, 256), 256)
        grad = dot(docs_t[...], delta[:, columns], ((1,), (0,))) * scale
        at = pl.ds(pl.multiple_of((t % 2) * 256, 256), 256)
        gc[:, :, t // 2, :, at] = grad.astype(BF16).reshape(NY, NC, 128, 256)
        return carry

    scores_one(sib[3:4], far)
    c_core = []
    for g in range(NX):
        lax.fori_loop(2 * g, 2 * g + 2, grad_one, 0)
        c_core.append(
            cp.start(gc.at[pl.ds(0, NY), 1 - c, g], c_in.at[pl.ds(0, NY), g], me.at(dc=1))
        )

    along_x, along_y = (lambda i: me.at(dx=i)), (lambda i: me.at(dy=i))
    a_rows, b_rows = pl.ds(0, 64), pl.ds(64, 64)
    blocks = Chain(cp, along_y, lambda k, at: gb.at[(y + k) % NY, c, at], by_2, by_s, by_r, 512)
    first_a = Chain(cp, along_y, lambda k, at: gc.at[(y + k) % NY, c, at, a_rows], fa_2, fa_s, fa_r)
    first_b = Chain(cp, along_x, lambda k, at: gc.at[at, c, k, b_rows], fb_2, fb_s, fb_r)
    then_a = Chain(cp, along_x, lambda k, at: c_a.at[k, at], ga_2, ga_s, ga_r, 16)
    then_b = Chain(cp, along_y, lambda k, at: c_b.at[(y + k) % NY, at], gb_2, gb_s, gb_r, 16)

    for copy in b_core:
        copy.wait_recv()

    def add_block(i, carry):
        rows = pl.ds(pl.multiple_of((i % 4) * 512, 512), 512)
        gb[i // 4, c, rows] = (gb[i // 4, c, rows].astype(F32) + b_in[i // 4, rows].astype(F32)).astype(BF16)
        return carry

    lax.fori_loop(0, 16, add_block, 0)
    blocks.begin()

    def hidden_one(t, carry):
        columns = pl.ds(pl.multiple_of(t * 256, 256), 256)
        weight = wrel[:, :, :, :, columns].reshape(NX * CL, 256)
        hid[:, :, columns] = dot(delta[...], weight, ((1,), (0,))).reshape(NZ, DOC, 256)
        return carry

    lax.fori_loop(0, 2, hidden_one, 0)
    for copy in c_core:
        copy.wait_recv()

    def add_cluster(i, carry):
        t, g = i // 4, i % 4
        gc[t, c, g] = (gc[t, c, g].astype(F32) + c_in[t, g].astype(F32)).astype(BF16)
        return carry

    lax.fori_loop(0, 16, add_cluster, 0)
    first_a.begin()
    first_b.begin()
    lax.fori_loop(2, 4, hidden_one, 0)

    def combine(i):
        t = (z + i) % NZ
        for copy in returns[i % NZ]:
            copy.wait_recv()
        hid[t] = hid[t] + dot(place[t], ret[t], ((0,), (0,)))

    z_right, z_left = [None, None], [None, None]
    parts = (slice(0, D // 2), slice(D // 2, D))

    def z_send(h, p):
        z_right[p] = cp.start(zs_r.at[h - 1, p], zr_r.at[h - 1, p], me.at(dz=1))
        z_left[p] = cp.start(zs_l.at[h - 1, p], zr_l.at[h - 1, p], me.at(dz=-1))

    def z_step(h):
        right, left = (z + h) % NZ, (z - h) % NZ
        combine(h)
        combine(-h)
        for p, cols in enumerate(parts):
            z_right[p].wait_recv()
            z_left[p].wait_recv()
            if h == 3:
                zs_r[2, p, 0:half] = (hid[right, 0:half, cols] + zr_r[3, p, 0:half].astype(F32)).astype(BF16)
                zs_r[2, p, half:DOC] = hid[right, half:DOC, cols].astype(BF16)
                zs_l[2, p, half:DOC] = (hid[left, half:DOC, cols] + zr_l[3, p, half:DOC].astype(F32)).astype(BF16)
                zs_l[2, p, 0:half] = hid[left, 0:half, cols].astype(BF16)
            else:
                zs_r[h - 1, p] = (hid[right, :, cols] + zr_r[h, p].astype(F32)).astype(BF16)
                zs_l[h - 1, p] = (hid[left, :, cols] + zr_l[h, p].astype(F32)).astype(BF16)
            z_send(h, p)

    combine(4)
    for p, cols in enumerate(parts):
        zs_r[3, p, 0:half] = hid[opposite, 0:half, cols].astype(BF16)
        zs_l[3, p, half:DOC] = hid[opposite, half:DOC, cols].astype(BF16)
        z_right[p] = cp.start(zs_r.at[3, p, halves[0]], zr_r.at[3, p, halves[0]], me.at(dz=1))
        z_left[p] = cp.start(zs_l.at[3, p, halves[1]], zr_l.at[3, p, halves[1]], me.at(dz=-1))

    def put(ref):
        def store(at, value):
            ref[at] = value.astype(ref.dtype)

        return store

    def put_b(at, value):
        o_c[pl.ds(64 + at.start, at.size)] = value

    blocks.middle()
    z_step(3)
    first_a.middle()
    z_step(2)
    first_b.middle()
    z_step(1)
    blocks.end(put(o_b))
    done_b = pltpu.make_async_copy(o_b, out_b, local.at[7])
    done_b.start()
    combine(0)
    first_b.end(put(c_b))
    then_b.begin()
    first_a.end(put(c_a))
    then_a.begin()
    then_b.middle()
    then_a.middle()
    for p, cols in enumerate(parts):
        z_right[p].wait_recv()
        z_left[p].wait_recv()
        o_h[:, cols] = (hid[z, :, cols] + zr_r[0, p].astype(F32) + zr_l[0, p].astype(F32)).astype(BF16)
    done_h = pltpu.make_async_copy(o_h, out_h, local.at[8])
    done_h.start()
    then_b.end(put_b)
    then_a.end(put(o_c))
    done_c = pltpu.make_async_copy(o_c, out_c, local.at[6])
    done_c.start()
    for copy in (done_c, done_b, done_h):
        copy.wait()
    cp.finish()


def w_part(wrel, group, y, c, part):
    return wrel.at[group, y, c, pl.ds(part * 32, 32)]


def per_device(encoded, positive_clusters, cluster_weight, shortlist, positive_offsets, block_weight):
    vmem = pl.BlockSpec(memory_space=pltpu.VMEM)
    hbm = pl.BlockSpec(memory_space=pl.ANY)
    bf = lambda *shape: pltpu.VMEM(shape, BF16)
    f32 = lambda *shape: pltpu.VMEM(shape, F32)
    copies = 128
    out_h, out_c, out_b = pl.pallas_call(
        kernel,
        out_shape=(
            jax.ShapeDtypeStruct((DOC, D), BF16),
            jax.ShapeDtypeStruct((128, CL), F32),
            jax.ShapeDtypeStruct((2048, 128), F32),
        ),
        in_specs=[hbm] * 6,
        out_specs=(hbm,) * 3,
        scratch_shapes=[
            bf(NZ, DOC, D), bf(D, NZ * DOC), bf(NX, NY, NC, 64, D), bf(16, LBL, D),
            pltpu.VMEM((NZ, 16, 128), jnp.int32), f32(NZ * DOC, 16), bf(NX, NZ, 32, D), f32(NX, NZ, 128),
            f32(16, 64), bf(NZ, 128, 128), bf(NZ, 128, D), bf(16, 64, D), bf(NZ * DOC, NX * CL),
            bf(NZ, 128, D), f32(NZ, DOC, D), bf(4, 2, DOC, D // 2), bf(4, 2, DOC, D // 2), bf(4, 2, DOC, D // 2),
            bf(4, 2, DOC, D // 2),
            bf(NY, NC, NX, 128, CL), bf(NY, NX, 128, CL),
            bf(4, 64, CL), bf(2, 4, 64, CL), bf(2, 4, 64, CL), bf(4, 64, CL), bf(2, 4, 64, CL), bf(2, 4, 64, CL),
            bf(4, 64, CL), bf(4, 64, CL), bf(64, CL), bf(2, 64, CL), bf(2, 64, CL), bf(64, CL), bf(2, 64, CL), bf(2, 64, CL),
            bf(NY, NC, 2048, 128), bf(NY, 2048, 128), bf(2048, 128), bf(2, 2048, 128), bf(2, 2048, 128),
            bf(DOC, D), f32(128, CL), f32(2048, 128),
            pltpu.SemaphoreType.DMA((copies,)),
            pltpu.SemaphoreType.DMA((copies,)),
            pltpu.SemaphoreType.DMA((9,)),
        ],
        compiler_params=pltpu.CompilerParams(
            collective_id=0, has_side_effects=True, vmem_limit_bytes=VMEM_LIMIT
        ),
    )(
        encoded, cluster_weight.reshape(NY, NC, 64, D), positive_clusters.T, shortlist.T,
        positive_offsets.T, block_weight,
    )
    out_h, out_c, out_b = pl.pallas_call(
        place_kernel,
        out_shape=(
            jax.ShapeDtypeStruct((DOC, D), BF16),
            jax.ShapeDtypeStruct((CL, 128), F32),
            jax.ShapeDtypeStruct((2048, 128), F32),
        ),
        in_specs=[vmem] * 3,
        out_specs=(vmem,) * 3,
    )(out_h, out_c, out_b)
    return out_h, out_c, out_b.reshape(16, LBL, 128)


def place_kernel(in_h, in_c, in_b, out_h, out_c, out_b):
    out_h[...] = in_h[...]
    out_c[...] = jnp.transpose(in_c[...], (1, 0))
    out_b[...] = in_b[...]


def solution(mesh):
    placed = (
        P(("dp", "label"), None),
        P(("dp", "label"), None),
        P("label", None),
        P(("dp", "label"), None),
        P(("dp", "label"), None),
        P("label", None, None),
    )
    return jax.shard_map(
        per_device,
        mesh=mesh,
        in_specs=placed,
        out_specs=(P(("dp", "label"), None), P("label", "dp"), P("label", None, "dp")),
        check_vma=False,
    )
```

time: 102 us -> 96.2 us (0.943)
  Pallas kernels: 101 us -> 95.5 us
    pallas_call x1, Pallas kernels: 98.7 us -> 92.9 us  [per_device(): pl.pallas_call(kernel, out_shape=(jax.ShapeDtypeStruct((DOC, D), BF16), j...]
where the time goes in v4:
time: 96.2 us; the launch traced here: 96.1 us
  Pallas kernels  95.5 us (99%)
    pallas_call x1, Pallas kernels, per_device(): pl.pallas_call(kernel, out_shape=(jax.ShapeDtypeStruct((DOC, D), BF16), j...  92.9 us
    pallas_call x1, Pallas kernels, per_device(): pl.pallas_call(place_kernel, out_shape=(jax.ShapeDtypeStruct((DOC, D), BF...  2.61 us

profile of v4, /device:TPU:2, one launch (start us, length us, event | category | flops | bytes accessed | tf_op | source)
XLA Modules:
  0.0 96.1 jit_solution(11509469010325442047)
XLA Ops:
  0.6 92.9 %shard_map.85 = (bf16[128,1024]{1,0:T(8,128)(2,1)}, f32[128,512]{1,0:T(8,128)}, f32[2048,128]{1,0:T(8,128)}) custom-call(bf16[128,1024]{1,0:T(8,128)(2,1)} %enc.1, bf16[4,2,64,1024]{3,2,1,0:T(8,128)(2,1)} %bitcast.5, s32[4,128]{1,0:T(4,128)} %bitcast.6, s32[4,128]{1,0:T(4,128)} %bitcast.7, s32[4,128]{1,0:T(4,128)} %bitcast.8, bf16[16,128,1024]{2,1,0:T(8,128)(2,1)} %bw_hbm.1), custom_call_target="tpu_custom_call" | custom-call | tf_op jit(solution)/shard_map/pallas_call | solution.py:466
  93.5 2.6 %shard_map.86 = (bf16[128,1024]{1,0:T(8,128)(2,1)}, f32[512,128]{1,0:T(8,128)}, f32[2048,128]{1,0:T(8,128)}) custom-call(bf16[128,1024]{1,0:T(8,128)(2,1)} %get-tuple-element.9.in_h, f32[128,512]{1,0:T(8,128)} %get-tuple-element.10.in_c, f32[2048,128]{1,0:T(8,128)} %get-tuple-element.11.in_b), custom_call_target="tpu_custom_call" | custom-call | tf_op jit(solution)/shard_map/pallas_call | solution.py:497

commit v5 on v4

--- a/solution.py
+++ b/solution.py
@@ -314,11 +314,15 @@
         rows = dot(shuffle, rows_p[:, e * 16:(e + 1) * 16, :].reshape(256, D), ((0,), (0,)))
         arr[e] = rows.astype(BF16).reshape(NZ, 32, D)
     returns = [[] for _ in range(NZ)]
-    for i in (4, 3, -3, 2, -2, 1, -1, 0):
+
+    def send_back(i):
         t = (z + i) % NZ
         for e in (2, 1, 3):
             dst = ret.at[t, pl.ds((NX - e) * 32, 32)]
             returns[i % NZ].append(cp.start(arr.at[e, t], dst, me.at(dx=e)))
+
+    for i in (4, 3, -3, 2, -2):
+        send_back(i)
     for i in range(NZ):
         ret[i, 0:32] = arr[0, i]
 
@@ -328,14 +332,6 @@
         at = pl.ds(pl.multiple_of((t % 2) * 256, 256), 256)
         gc[:, :, t // 2, :, at] = grad.astype(BF16).reshape(NY, NC, 128, 256)
         return carry
-
-    scores_one(sib[3:4], far)
-    c_core = []
-    for g in range(NX):
-        lax.fori_loop(2 * g, 2 * g + 2, grad_one, 0)
-        c_core.append(
-            cp.start(gc.at[pl.ds(0, NY), 1 - c, g], c_in.at[pl.ds(0, NY), g], me.at(dc=1))
-        )
 
     along_x, along_y = (lambda i: me.at(dx=i)), (lambda i: me.at(dy=i))
     a_rows, b_rows = pl.ds(0, 64), pl.ds(64, 64)
@@ -345,6 +341,7 @@
     then_a = Chain(cp, along_x, lambda k, at: c_a.at[k, at], ga_2, ga_s, ga_r, 16)
     then_b = Chain(cp, along_y, lambda k, at: c_b.at[(y + k) % NY, at], gb_2, gb_s, gb_r, 16)
 
+    scores_one(sib[3:4], far)
     for copy in b_core:
         copy.wait_recv()
 
@@ -362,25 +359,12 @@
         hid[:, :, columns] = dot(delta[...], weight, ((1,), (0,))).reshape(NZ, DOC, 256)
         return carry
 
-    lax.fori_loop(0, 2, hidden_one, 0)
-    for copy in c_core:
-        copy.wait_recv()
-
-    def add_cluster(i, carry):
-        t, g = i // 4, i % 4
-        gc[t, c, g] = (gc[t, c, g].astype(F32) + c_in[t, g].astype(F32)).astype(BF16)
-        return carry
-
-    lax.fori_loop(0, 16, add_cluster, 0)
-    first_a.begin()
-    first_b.begin()
-    lax.fori_loop(2, 4, hidden_one, 0)
-
-    def combine(i):
+    def combine(i, cols=slice(0, D), wait=True):
         t = (z + i) % NZ
-        for copy in returns[i % NZ]:
-            copy.wait_recv()
-        hid[t] = hid[t] + dot(place[t], ret[t], ((0,), (0,)))
+        if wait:
+            for copy in returns[i % NZ]:
+                copy.wait_recv()
+        hid[t, :, cols] = hid[t, :, cols] + dot(place[t], ret[t, :, cols], ((0,), (0,)))
 
     z_right, z_left = [None, None], [None, None]
     parts = (slice(0, D // 2), slice(D // 2, D))
@@ -406,38 +390,62 @@
                 zs_l[h - 1, p] = (hid[left, :, cols] + zr_l[h, p].astype(F32)).astype(BF16)
             z_send(h, p)
 
-    combine(4)
+    c_core = []
+
+    def grad_of(g):
+        lax.fori_loop(2 * g, 2 * g + 2, grad_one, 0)
+        c_core.append(
+            cp.start(gc.at[pl.ds(0, NY), 1 - c, g], c_in.at[pl.ds(0, NY), g], me.at(dc=1))
+        )
+
+    def add_cluster(i, carry):
+        t, g = i // 4, i % 4
+        gc[t, c, g] = (gc[t, c, g].astype(F32) + c_in[t, g].astype(F32)).astype(BF16)
+        return carry
+
+    def put(ref):
+        def store(at, value):
+            ref[at] = value.astype(ref.dtype)
+
+        return store
+
+    def put_b(at, value):
+        o_c[pl.ds(64 + at.start, at.size)] = value
+
+    for g in range(NX):
+        grad_of(g)
+    for copy in c_core:
+        copy.wait_recv()
+    lax.fori_loop(0, 16, add_cluster, 0)
+    first_a.begin()
+    first_b.begin()
     for p, cols in enumerate(parts):
+        lax.fori_loop(2 * p, 2 * p + 2, hidden_one, 0)
+        combine(4, cols, p == 0)
         zs_r[3, p, 0:half] = hid[opposite, 0:half, cols].astype(BF16)
         zs_l[3, p, half:DOC] = hid[opposite, half:DOC, cols].astype(BF16)
         z_right[p] = cp.start(zs_r.at[3, p, halves[0]], zr_r.at[3, p, halves[0]], me.at(dz=1))
         z_left[p] = cp.start(zs_l.at[3, p, halves[1]], zr_l.at[3, p, halves[1]], me.at(dz=-1))
-
-    def put(ref):
-        def store(at, value):
-            ref[at] = value.astype(ref.dtype)
-
-        return store
-
-    def put_b(at, value):
-        o_c[pl.ds(64 + at.start, at.size)] = value
-
+    send_back(1)
+    send_back(-1)
+    first_a.middle()
+    z_step(3)
     blocks.middle()
-    z_step(3)
-    first_a.middle()
+    first_b.middle()
+    send_back(0)
     z_step(2)
-    first_b.middle()
+    first_a.end(put(c_a))
+    then_a.begin()
     z_step(1)
+    then_a.middle()
+    first_b.end(put(c_b))
+    then_b.begin()
     blocks.end(put(o_b))
     done_b = pltpu.make_async_copy(o_b, out_b, local.at[7])
     done_b.start()
     combine(0)
-    first_b.end(put(c_b))
-    then_b.begin()
-    first_a.end(put(c_a))
-    then_a.begin()
+    then_a.end(put(o_c))
     then_b.middle()
-    then_a.middle()
     for p, cols in enumerate(parts):
         z_right[p].wait_recv()
         z_left[p].wait_recv()
@@ -445,7 +453,6 @@
     done_h = pltpu.make_async_copy(o_h, out_h, local.at[8])
     done_h.start()
     then_b.end(put_b)
-    then_a.end(put(o_c))
     done_c = pltpu.make_async_copy(o_c, out_c, local.at[6])
     done_c.start()
     for copy in (done_c, done_b, done_h):

time: 96.2 us -> 94.5 us (0.982)
  Pallas kernels: 95.5 us -> 93.6 us
    pallas_call x1, Pallas kernels: 92.9 us -> 91 us  [per_device(): pl.pallas_call(kernel, out_shape=(jax.ShapeDtypeStruct((DOC, D), BF16), j...]
where the time goes in v5:
time: 94.5 us; the launch traced here: 94.3 us
  Pallas kernels  93.6 us (99%)
    pallas_call x1, Pallas kernels, per_device(): pl.pallas_call(kernel, out_shape=(jax.ShapeDtypeStruct((DOC, D), BF16), j...  91 us
    pallas_call x1, Pallas kernels, per_device(): pl.pallas_call(place_kernel, out_shape=(jax.ShapeDtypeStruct((DOC, D), BF...  2.61 us

profile of v5, /device:TPU:2, one launch (start us, length us, event | category | flops | bytes accessed | tf_op | source)
XLA Modules:
  0.0 94.3 jit_solution(9240683685036498588)
XLA Ops:
  0.6 91.0 %shard_map.85 = (bf16[128,1024]{1,0:T(8,128)(2,1)}, f32[128,512]{1,0:T(8,128)}, f32[2048,128]{1,0:T(8,128)}) custom-call(bf16[128,1024]{1,0:T(8,128)(2,1)} %enc.1, bf16[4,2,64,1024]{3,2,1,0:T(8,128)(2,1)} %bitcast.5, s32[4,128]{1,0:T(4,128)} %bitcast.6, s32[4,128]{1,0:T(4,128)} %bitcast.7, s32[4,128]{1,0:T(4,128)} %bitcast.8, bf16[16,128,1024]{2,1,0:T(8,128)(2,1)} %bw_hbm.1), custom_call_target="tpu_custom_call" | custom-call | tf_op jit(solution)/shard_map/pallas_call | solution.py:473
  91.7 2.6 %shard_map.86 = (bf16[128,1024]{1,0:T(8,128)(2,1)}, f32[512,128]{1,0:T(8,128)}, f32[2048,128]{1,0:T(8,128)}) custom-call(bf16[128,1024]{1,0:T(8,128)(2,1)} %get-tuple-element.9.in_h, f32[128,512]{1,0:T(8,128)} %get-tuple-element.10.in_c, f32[2048,128]{1,0:T(8,128)} %get-tuple-element.11.in_b), custom_call_target="tpu_custom_call" | custom-call | tf_op jit(solution)/shard_map/pallas_call | solution.py:504

commit v6 on v5

--- a/solution.py
+++ b/solution.py
@@ -437,14 +437,10 @@
     first_a.end(put(c_a))
     then_a.begin()
     z_step(1)
-    then_a.middle()
     first_b.end(put(c_b))
     then_b.begin()
-    blocks.end(put(o_b))
-    done_b = pltpu.make_async_copy(o_b, out_b, local.at[7])
-    done_b.start()
+    then_a.middle()
     combine(0)
-    then_a.end(put(o_c))
     then_b.middle()
     for p, cols in enumerate(parts):
         z_right[p].wait_recv()
@@ -452,6 +448,10 @@
         o_h[:, cols] = (hid[z, :, cols] + zr_r[0, p].astype(F32) + zr_l[0, p].astype(F32)).astype(BF16)
     done_h = pltpu.make_async_copy(o_h, out_h, local.at[8])
     done_h.start()
+    then_a.end(put(o_c))
+    blocks.end(put(o_b))
+    done_b = pltpu.make_async_copy(o_b, out_b, local.at[7])
+    done_b.start()
     then_b.end(put_b)
     done_c = pltpu.make_async_copy(o_c, out_c, local.at[6])
     done_c.start()

time: 94.5 us -> 93.5 us (0.989)
  no operation moved by 1% of the time
where the time goes in v6:
time: 93.5 us; the launch traced here: 93.4 us
  Pallas kernels  92.7 us (99%)
    pallas_call x1, Pallas kernels, per_device(): pl.pallas_call(kernel, out_shape=(jax.ShapeDtypeStruct((DOC, D), BF16), j...  90.1 us
    pallas_call x1, Pallas kernels, per_device(): pl.pallas_call(place_kernel, out_shape=(jax.ShapeDtypeStruct((DOC, D), BF...  2.61 us

profile of v6, /device:TPU:2, one launch (start us, length us, event | category | flops | bytes accessed | tf_op | source)
XLA Modules:
  0.0 93.4 jit_solution(7303855570941416349)
XLA Ops:
  0.6 90.1 %shard_map.85 = (bf16[128,1024]{1,0:T(8,128)(2,1)}, f32[128,512]{1,0:T(8,128)}, f32[2048,128]{1,0:T(8,128)}) custom-call(bf16[128,1024]{1,0:T(8,128)(2,1)} %enc.1, bf16[4,2,64,1024]{3,2,1,0:T(8,128)(2,1)} %bitcast.5, s32[4,128]{1,0:T(4,128)} %bitcast.6, s32[4,128]{1,0:T(4,128)} %bitcast.7, s32[4,128]{1,0:T(4,128)} %bitcast.8, bf16[16,128,1024]{2,1,0:T(8,128)(2,1)} %bw_hbm.1), custom_call_target="tpu_custom_call" | custom-call | tf_op jit(solution)/shard_map/pallas_call | solution.py:473
  90.8 2.6 %shard_map.86 = (bf16[128,1024]{1,0:T(8,128)(2,1)}, f32[512,128]{1,0:T(8,128)}, f32[2048,128]{1,0:T(8,128)}) custom-call(bf16[128,1024]{1,0:T(8,128)(2,1)} %get-tuple-element.9.in_h, f32[128,512]{1,0:T(8,128)} %get-tuple-element.10.in_c, f32[2048,128]{1,0:T(8,128)} %get-tuple-element.11.in_b), custom_call_target="tpu_custom_call" | custom-call | tf_op jit(solution)/shard_map/pallas_call | solution.py:504
